TPU v7x, 32 devices: a whole 2x2x4 slice. The times are simulated.
32 devices in a mesh: cells: 8 (over z, x), vecs: 4 (over y, core).
Axes of the slice: x: 2, y: 2, z: 4, core: 2. Of those that a mesh axis runs over, the one named last changes fastest.
Arguments:
- wave_block: float32 [64, 73728], P('vecs', 'cells'), may hold values from -6 to 6
- connectivity: int32 [125, 1024], P(None, 'cells'), may hold values from 0 to 10304, as said below
- send_list: int32 [8712], P('cells'), may hold values from 0 to 9215, as said below
- levels: int32 [1024], P('cells'), may hold values from 0 to 2
- live_cells: int32 [8], P('cells'), may hold values from 64 to 128, as said below
- potential: float32 [125, 1024], P(None, 'cells'), may hold values from -24 to 8
- mass_scale: float32 [73728], P('cells'), may hold values from 0.5 to 2
- center: float32 [], replicated, may hold values from 20 to 30
- halfwidth: float32 [], replicated, may hold values from 25 to 35
- earlier_vectors: bfloat16 [2048, 73728], P(None, ('cells', 'vecs')), may hold values from -0.0234375 to 0.0234375
Outputs:
- filtered: float32 [64, 73728], P(None, ('cells', 'vecs'))
- projections: float32 [2048, 64], P(('cells', 'vecs'))
Inputs may be any that keep to these rules, and one draw needn't show every extreme that they name: `connectivity`: column c names the slots of cell c's 125 nodes on its device, node (a,b,c) of the reference cube at row 25 a + 5 b + c. A device's cells form a structured block of 8 x 8 x 2 cells of degree 4 in Morton order, nodes numbered at random over the 9216 node slots; the face of the block toward the device before it lies in the ghost slots 9216 to 10304 in the order of that device's send_list, so that exactly 64 cells of each device name ghost slots. `send_list`: A device's 1089 entries are distinct node slots of its block's face toward the device after it. Cells 0 to live_cells - 1 of a device are in use, the rest of its slots are empty; some device uses all 128, some only 64.
All inputs are finite; a program needn't handle non-finite values.
Results may differ from a plain program's by a relative error of at most 0.0031.
Values may be sent and summed in bfloat16 or wider, within the bound.
A program may use at most 128 MiB of HBM per device.

v0:
```python
import math

import jax
import jax.numpy as jnp
import numpy as np
from jax import lax
from jax.sharding import PartitionSpec as P


def passed_along(value, axis, steps):
    count = lax.axis_size(axis)
    leading, last = (max(0, -steps), min(count, count - steps))
    return lax.ppermute(value, axis, [(source, source + steps) for source in range(leading, last)])


def gll_tables():
    root_value = math.sqrt(3.0 / 7.0)
    points = np.array([-1.0, -root_value, 0.0, root_value, 1.0])
    weights = np.array([0.1, 49.0 / 90.0, 32.0 / 45.0, 49.0 / 90.0, 0.1])
    barycentric = np.ones(5)
    for node_index in range(5):
        for other_node in range(5):
            if other_node != node_index:
                barycentric[node_index] = barycentric[node_index] / (
                    points[node_index] - points[other_node]
                )
    derivative = np.zeros((5, 5))
    for row_index in range(5):
        for col_index in range(5):
            if row_index != col_index:
                derivative[row_index, col_index] = (
                    barycentric[col_index]
                    / barycentric[row_index]
                    / (points[row_index] - points[col_index])
                )
        derivative[row_index, row_index] = -np.sum(derivative[row_index])
    mass_one = np.zeros((5, 5))
    for node_index in range(5):
        mass_one[node_index, node_index] = weights[node_index]
    laplace_one = derivative.T @ mass_one @ derivative
    stiffness = (
        np.kron(np.kron(laplace_one, mass_one), mass_one)
        + np.kron(np.kron(mass_one, laplace_one), mass_one)
        + np.kron(np.kron(mass_one, mass_one), laplace_one)
    )
    quadrature = np.kron(np.kron(weights, weights), weights)
    return (stiffness.astype(np.float32), quadrature.astype(np.float32))


def per_device(
    wave_block,
    connectivity,
    send_list,
    levels,
    live_cells,
    potential,
    mass_scale,
    center,
    halfwidth,
    earlier_vectors,
):
    stiffness, quadrature = gll_tables()
    stiffness_low = jnp.asarray(stiffness).astype(jnp.bfloat16)
    quad_weights = jnp.asarray(quadrature).astype(jnp.float32)
    columns = wave_block.shape[0]
    owned_count = wave_block.shape[1]
    ghost_count = send_list.shape[0]
    cell_count = connectivity.shape[1]
    cell_size = jnp.exp2(-levels.astype(jnp.float32))
    in_use = (jnp.arange(cell_count, dtype=jnp.int32) < live_cells[0]).astype(jnp.float32)
    kinetic = cell_size / 4.0 * in_use
    volume = cell_size**3 / 8.0 * in_use
    coefficient = volume[None, :] * quad_weights[:, None] * potential

    def cell_sum(extended, cells_conn, kin_part, coeff_part):
        values = extended[:, cells_conn].astype(jnp.bfloat16)
        stiff_part = jnp.einsum(
            "jk,vkc->vjc", stiffness_low, values, preferred_element_type=jnp.float32
        )
        cell_terms = kin_part[None, None, :] * stiff_part + coeff_part[None] * values.astype(
            jnp.float32
        )
        return (
            jnp.zeros((columns, owned_count + ghost_count), jnp.float32)
            .at[:, cells_conn]
            .add(cell_terms)
        )

    def apply_operator(vectors):
        scaled = vectors * mass_scale[None, :]
        top_face = scaled[:, send_list]
        ghosts = passed_along(top_face.astype(jnp.bfloat16), "cells", 1).astype(top_face.dtype)
        extended = jnp.concatenate([scaled, ghosts], 1)
        slot_sums = cell_sum(extended, connectivity, kinetic, coefficient)
        returned = passed_along(
            slot_sums[:, owned_count:].astype(jnp.bfloat16), "cells", -1
        ).astype(jnp.float32)
        summed = slot_sums[:, :owned_count].at[:, send_list].add(returned)
        return summed * mass_scale[None, :]

    degree_one = (apply_operator(wave_block) - center * wave_block) / halfwidth
    degree_two = 2.0 * (apply_operator(degree_one) - center * degree_one) / halfwidth - wave_block
    rounded = degree_two.astype(jnp.bfloat16)
    quarter = lax.all_to_all(rounded, "vecs", split_axis=1, concat_axis=0, tiled=True)
    row_share = earlier_vectors.shape[0] // lax.axis_size(("cells", "vecs"))
    partial_sum = lax.dot_general(
        earlier_vectors, quarter, (((1,), (1,)), ((), ())), preferred_element_type=jnp.float32
    )
    projections = lax.psum(partial_sum, ("cells", "vecs"))
    filtered = quarter.astype(jnp.float32) - lax.dot_general(
        projections.astype(jnp.bfloat16),
        earlier_vectors,
        (((0,), (0,)), ((), ())),
        preferred_element_type=jnp.float32,
    )
    own_rows = lax.dynamic_slice_in_dim(
        projections, lax.axis_index(("cells", "vecs")) * row_share, row_share, 0
    )
    return (filtered, own_rows)


def solution(mesh):
    in_specs = (
        P("vecs", "cells"),
        P(None, "cells"),
        P("cells"),
        P("cells"),
        P("cells"),
        P(None, "cells"),
        P("cells"),
        P(),
        P(),
        P(None, ("cells", "vecs")),
    )
    out_specs = (P(None, ("cells", "vecs")), P(("cells", "vecs"), None))
    return jax.shard_map(
        per_device, mesh=mesh, in_specs=in_specs, out_specs=out_specs, check_vma=False
    )
```

profile of v0, /device:TPU:0, one launch (start us, length us, event | category | flops | bytes accessed | tf_op | source)
XLA Modules:
  0.0 525.8 jit_solution(17471628490798330622)
XLA Ops:
  7.2 0.7 compare_select_fusion.1
  7.9 1.1 broadcast_multiply_fusion.1
  9.0 1.1 copy.91
  10.2 2.9 gather_fusion
  13.2 4.9 collective-permute-start
  18.1 0.9 fusion.19
  19.6 0.7 compare_select_fusion.3
  20.2 0.9 multiply_multiply_fusion
  21.3 2.1 copy.93
  23.5 32.9 %gather_fusion.1 = bf16[16000,16]{1,0:T(8,128)(2,1)} fusion(bf16[16,10305]{0,1:T(8,128)(2,1)S(1)} %copy.93, s32[16384]{0:T(1024)S(1)} %pad_clamp_fusion), kind=kCustom, calls=%fused_computation.1 | custom fusion | bytes 1088000 | tf_op jit(solution)/shard_map/gather | solution.py:76
  56.4 3.7 copy.94
  60.1 0.3 reshape.88
  60.4 0.3 copy.95
  60.7 0.3 fusion.9
  61.0 7.5 %copy.110 = f32[125,128,16]{2,1,0:T(8,128)} copy(f32[125,128,16]{0,1,2:T(8,128)S(1)} %fusion.9) | data formatting | bytes 2048000 | tf_op jit(solution)/shard_map/add | solution.py:80
  68.5 90.6 %scatter_custom_fusion = f32[16,10305]{0,1:T(8,128)} fusion(s32[16000]{0:T(1024)S(1)} %fusion.19, f32[16000,16]{1,0:T(8,128)} %bitcast.60, f32[]{:T(128)} %constant.16.clone.1), kind=kCustom, calls=%fused_computation.11 | custom fusion | flops 256000 | bytes 660032 | tf_op jit(solution)/shard_map/scatter-add | solution.py:86
  159.2 1.1 slice.33
  160.3 1.3 collective-permute-start.1
  162.9 3.9 slice.26
  166.8 3.5 collective-permute-done.1
  170.3 13.8 %scatter_custom_fusion.1 = f32[16,9216]{0,1:T(8,128)} fusion(f32[16,9216]{0,1:T(8,128)} %slice.26, s32[1089]{0:T(1024)S(1)} %compare_select_fusion.1, bf16[16,1089]{0,1:T(8,128)(2,1)S(1)} %collective-permute-done.1), kind=kCustom, calls=%fused_computation.30 | custom fusion | flops 34848 | bytes 870400 | tf_op jit(solution)/shard_map/scatter-add | solution.py:98
  184.1 3.0 copy.99
  187.3 1.9 copy.100
  189.2 4.4 gather_fusion.2
  193.7 4.4 collective-permute-start.2
  198.1 1.6 collective-permute-done.2
  199.7 0.7 pad_maximum_fusion.1
  200.5 2.7 copy.102
  203.2 32.9 %gather_fusion.3 = bf16[16000,16]{1,0:T(8,128)(2,1)} fusion(bf16[16,10305]{0,1:T(8,128)(2,1)S(1)} %copy.102, s32[16384]{0:T(1024)S(1)} %pad_clamp_fusion), kind=kCustom, calls=%fused_computation.3 | custom fusion | bytes 1088000 | tf_op jit(solution)/shard_map/gather | solution.py:76
  236.1 3.7 copy.103
  239.9 0.3 reshape.89
  240.1 0.3 copy.104
  240.4 0.3 fusion.6
  240.8 7.5 %copy.111 = f32[125,128,16]{2,1,0:T(8,128)} copy(f32[125,128,16]{0,1,2:T(8,128)S(1)} %fusion.6) | data formatting | bytes 2048000 | tf_op jit(solution)/shard_map/add | solution.py:80
  248.3 90.6 %scatter_custom_fusion.2 = f32[16,10305]{0,1:T(8,128)} fusion(s32[16000]{0:T(1024)S(1)} %fusion.19, f32[16000,16]{1,0:T(8,128)} %bitcast.59, f32[]{:T(128)} %constant.16.clone.1), kind=kCustom, calls=%fused_computation.9 | custom fusion | flops 256000 | bytes 660032 | tf_op jit(solution)/shard_map/scatter-add | solution.py:86
  338.9 1.1 slice.32
  340.0 1.3 collective-permute-start.3
  341.3 3.9 slice.28
  345.3 3.5 collective-permute-done.3
  348.8 13.8 %scatter_custom_fusion.3 = f32[16,9216]{0,1:T(8,128)} fusion(f32[16,9216]{0,1:T(8,128)} %slice.28, s32[1089]{0:T(1024)S(1)} %compare_select_fusion.1, bf16[16,1089]{0,1:T(8,128)(2,1)S(1)} %collective-permute-done.3), kind=kCustom, calls=%fused_computation.28 | custom fusion | flops 34848 | bytes 870400 | tf_op jit(solution)/shard_map/scatter-add | solution.py:98
  362.6 3.0 copy.107
  365.6 0.2 subtract_convert_fusion
  365.9 9.0 %all_to_all.19 = bf16[16,4,2304]{2,0,1:T(8,128)(2,1)S(1)} all-to-all(bf16[16,4,2304]{2,0,1:T(8,128)(2,1)S(1)} %bitcast.63), channel_id=1, replica_groups=mesh['cells'=8,'vecs'=4] {'vecs'}, dimensions={1} | all-to-all | bytes 589824 | tf_op jit(solution)/shard_map/all_to_all | solution.py:104
  374.8 7.4 %convolution_bitcast_fusion = f32[2048,64]{0,1:T(8,128)} fusion(bf16[64,2304]{1,0:T(8,128)(2,1)S(1)} %bitcast.61, bf16[2048,2304]{1,0:T(8,128)(2,1)} %param.21), kind=kOutput, calls=%fused_computation.13 | convolution fusion | flops 603979776 | bytes 10256384 | tf_op jit(solution)/shard_map/dot_general | solution.py:106
  382.3 128.8 %all-reduce.2.cloned.1.call-done = f32[2048,64]{0,1:T(8,128)} async-done(((f32[2048,64]{0,1:T(8,128)}), f32[2048,64]{0,1:T(8,128)}) %all-reduce.2.cloned.1.call-update) | async-done | bytes 524304 | tf_op jit(solution)/shard_map/psum | solution.py:109
  511.1 0.8 constant_dynamic-slice_fusion
  511.9 0.7 copy.109
  512.6 6.4 %convolution_subtract_fusion = f32[64,2304]{1,0:T(8,128)} fusion(bf16[2048,2304]{1,0:T(8,128)(2,1)} %param.21, bf16[64,2304]{1,0:T(8,128)(2,1)S(1)} %bitcast.62, f32[2048,64]{0,1:T(8,128)} %all-reduce.2.cloned.1.call-done), kind=kOutput, calls=%fused_computation.8 | convolution fusion | flops 604405760 | bytes 10846208 | tf_op jit(solution)/shard_map/dot_general | solution.py:110
  (21 shorter events, 0.7 us)
Async XLA Ops:
  7.2 503.9 %all-reduce.2.cloned.1.call-start = ((), (), s32[]{:S(2)}) async-start(), calls=%async_computation.1 | async-start | bytes 1048576 | tf_op jit(solution)/shard_map/psum | solution.py:109
  13.2 8.1 %collective-permute-start = (bf16[16,1089]{1,0:T(8,128)(2,1)S(1)}, bf16[16,1089]{1,0:T(8,128)(2,1)S(1)}, u32[]{:S(2)}, u32[]{:S(2)}) collective-permute-start(bf16[16,1089]{1,0:T(8,128)(2,1)S(1)} %bitcast.65), channel_id=1, source_target_pairs={{0,4},{4,8},{8,12},{12,16},{16,20},{20,24},{24,28},{1,5},{5,9},{9,... | collective-permute-start | bytes 104552 | tf_op jit(solution)/shard_map/ppermute | solution.py:13
  23.5 37.2 %copy-start.4 = (bf16[125,125,1]{1,0,2:T(8,128)(2,1)S(1)}, bf16[125,125,1]{1,0,2:T(8,128)(2,1)}, u32[]{:S(2)}) copy-start(bf16[125,125,1]{1,0,2:T(8,128)(2,1)} %constant.46) | copy-start | bytes 93754
  160.3 10.1 %collective-permute-start.1 = (bf16[16,1089]{0,1:T(8,128)(2,1)S(1)}, bf16[16,1089]{0,1:T(8,128)(2,1)S(1)}, u32[]{:S(2)}, u32[]{:S(2)}) collective-permute-start(bf16[16,1089]{0,1:T(8,128)(2,1)S(1)} %slice.33), channel_id=1, source_target_pairs={{4,0},{8,4},{12,8},{16,12},{20,16},{24,20},{28,24},{5,1},{9,5},{13... | collective-permute-start | bytes 104552 | tf_op jit(solution)/shard_map/ppermute | solution.py:13
  166.8 20.3 %copy-start = (f32[16,9216]{1,0:T(8,128)S(1)}, f32[16,9216]{1,0:T(8,128)}, u32[]{:S(2)}) copy-start(f32[16,9216]{1,0:T(8,128)} %param.12) | copy-start | bytes 1769476
  166.8 20.3 %copy-start.3 = (f32[9216]{0:T(1024)S(1)}, f32[9216]{0:T(1024)}, u32[]{:S(2)}) copy-start(f32[9216]{0:T(1024)} %param.18) | copy-start | bytes 110596
  187.1 12.6 %copy-start.1 = (f32[16,9216]{1,0:T(8,128)}, f32[16,9216]{1,0:T(8,128)S(1)}, u32[]{:S(2)}) copy-start(f32[16,9216]{1,0:T(8,128)S(1)} %copy.99) | copy-start | bytes 1769476
  193.7 6.0 %collective-permute-start.2 = (bf16[16,1089]{1,0:T(8,128)(2,1)S(1)}, bf16[16,1089]{1,0:T(8,128)(2,1)S(1)}, u32[]{:S(2)}, u32[]{:S(2)}) collective-permute-start(bf16[16,1089]{1,0:T(8,128)(2,1)S(1)} %bitcast.66), channel_id=1, source_target_pairs={{0,4},{4,8},{8,12},{12,16},{16,20},{20,24},{24,28},{1,5},{5,9},{9,... | collective-permute-start | bytes 104552 | tf_op jit(solution)/shard_map/ppermute | solution.py:13
  340.0 8.8 %collective-permute-start.3 = (bf16[16,1089]{0,1:T(8,128)(2,1)S(1)}, bf16[16,1089]{0,1:T(8,128)(2,1)S(1)}, u32[]{:S(2)}, u32[]{:S(2)}) collective-permute-start(bf16[16,1089]{0,1:T(8,128)(2,1)S(1)} %slice.32), channel_id=1, source_target_pairs={{4,0},{8,4},{12,8},{16,12},{20,16},{24,20},{28,24},{5,1},{9,5},{13... | collective-permute-start | bytes 104552 | tf_op jit(solution)/shard_map/ppermute | solution.py:13
  345.3 20.3 %copy-start.2 = (f32[16,9216]{1,0:T(8,128)S(1)}, f32[16,9216]{1,0:T(8,128)}, u32[]{:S(2)}) copy-start(f32[16,9216]{1,0:T(8,128)} %copy-done.1) | copy-start | bytes 1769476
Sparse Core Ops, SparseCore 0:
  382.4 128.6 all-reduce.1
where the time goes:
time: 527 us; the launch traced here: 526 us
  other arithmetic  214 us (41%)
  waiting for transfers between devices  137 us (26%)
  local copies, waits for them, and re-layouts  123 us (23%)
  between operations  16.2 us (3%)
  matrix products  14.4 us (3%)
  starting transfers between devices  11.8 us (2%)
  blocking collectives  8.98 us (2%)
    scatter-add x2, other arithmetic, cell_sum(): return jnp.zeros((columns, owned_count + ghost_count), jnp.float32).at[:,...  181 us
    psum x1, waiting for transfers between devices, per_device(): projections = lax.psum(partial_sum, ('cells', 'vecs'))  129 us
    gather x4, local copies, waits for them, and re-layouts, cell_sum(): values = extended[:, cells_conn].astype(jnp.bfloat16)  73.2 us
    scatter-add x2, other arithmetic, apply_operator(): summed = slot_sums[:, :owned_count].at[:, send_list].add(returned)  27.5 us
    add x2, local copies, waits for them, and re-layouts, cell_sum(): kin_part[None, None, :] * stiff_part  15.1 us
    ppermute x4, starting transfers between devices, passed_along(): lax.ppermute(value, axis, [(source, source + steps) for source in range(l...  11.8 us
  transfers between devices with their start and end apart: 5, of which 4 were waited for; matrix products, arithmetic and copies ran while one was open for 2% of the time, Pallas kernels for 0%

commit v1 on v0

--- a/solution.py
+++ b/solution.py
@@ -1,10 +1,17 @@
+import functools
 import math
 
 import jax
 import jax.numpy as jnp
 import numpy as np
 from jax import lax
+from jax.experimental import pallas as pl
+from jax.experimental.pallas import tpu as pltpu
 from jax.sharding import PartitionSpec as P
+
+ROWS = 200
+HALF = 63
+VMEM_BYTES = 48 * 1024 * 1024
 
 
 def passed_along(value, axis, steps):
@@ -47,6 +54,257 @@
     return (stiffness.astype(np.float32), quadrature.astype(np.float32))
 
 
+def fixed_tables():
+    stiffness, quadrature = gll_tables()
+    spread = np.zeros((208, 128), np.float32)
+    for j in range(125):
+        spread[8 * (j // 5) + j % 5, j] = 1.0
+    spread[200, 125] = 1.0
+    padded = spread[:200, :125] @ stiffness @ spread[:200, :125].T
+    reorder = np.zeros((128, 128), np.float32)
+    for rank in range(128):
+        bit = [rank >> k & 1 for k in range(7)]
+        x = bit[0] + 2 * bit[3] + 4 * bit[5]
+        y = bit[1] + 2 * bit[4] + 4 * bit[6]
+        reorder[rank, 64 * bit[2] + 8 * x + y] = 1.0
+    return padded, quadrature, spread, reorder
+
+
+def lane_iota(shape):
+    return lax.broadcasted_iota(jnp.int32, shape, 1)
+
+
+def row_iota(shape):
+    return lax.broadcasted_iota(jnp.int32, shape, 0)
+
+
+def gather_kernel(
+    wave, mass, conn_high, conn_low, cell_data, spread, reorder,
+    nodal, face, inverse, cell_out, packed, low, high, stage,
+):
+    chunks = wave.shape[1] // 256
+    vectors = wave.shape[0]
+    group = vectors + 8
+    order = reorder[...]
+    order_low = order.astype(jnp.bfloat16)
+    high[...] = jnp.dot(conn_high[...], order_low, preferred_element_type=jnp.float32).astype(jnp.int32)
+    low[...] = jnp.dot(conn_low[...], order_low, preferred_element_type=jnp.float32).astype(jnp.int32)
+    exact = lax.Precision.HIGHEST
+    ordered = jnp.dot(cell_data[...], order, precision=exact, preferred_element_type=jnp.float32)
+    cell_out[...] = jnp.dot(spread[...], ordered, precision=exact, preferred_element_type=jnp.float32)
+    for chunk in range(chunks):
+        columns = slice(256 * chunk, 256 * chunk + 256)
+        scale = mass[:, columns]
+        packed[group * chunk:group * chunk + vectors, :] = wave[:, columns] * scale
+        packed[group * chunk + vectors:group * chunk + group, :] = jnp.broadcast_to(scale, (8, 256))
+    value = packed[...]
+    value_high = value.astype(jnp.bfloat16)
+    value_low = (value - value_high.astype(jnp.float32)).astype(jnp.bfloat16)
+    stage[...] = jnp.zeros_like(stage)
+    inverse[...] = jnp.zeros_like(inverse)
+    lane = lane_iota((1, 128))
+    cell_z, cell_x, cell_y = lane >> 6, lane >> 3 & 7, lane & 7
+
+    def first_copy(j):
+        a, b, c = lax.div(j, 25), lax.rem(lax.div(j, 5), 5), lax.rem(j, 5)
+        keep_x = cell_x + jnp.where(a < 4, 7, 0) >= 7
+        keep_y = cell_y + jnp.where(b < 4, 7, 0) >= 7
+        keep_z = cell_z + jnp.where(c < 4, 1, 0) >= 1
+        kept = jnp.where(keep_x & keep_y & keep_z, 1, 0)
+        return kept * (j + 1), kept * lane
+
+    def step(i, carry):
+        j = 2 * i
+        slot_low = jnp.concatenate([low[pl.ds(j, 1), :], low[pl.ds(j + 1, 1), :]], axis=1)
+        slot_high = jnp.concatenate([high[pl.ds(j, 1), :], high[pl.ds(j + 1, 1), :]], axis=1)
+        one_hot = jnp.where(row_iota((256, 256)) == slot_low, 1.0, 0.0).astype(jnp.bfloat16)
+        product = jnp.dot(value_high, one_hot, preferred_element_type=jnp.float32)
+        product = product + jnp.dot(value_low, one_hot, preferred_element_type=jnp.float32)
+        total = jnp.zeros((group, 256), jnp.float32)
+        for chunk in range(chunks):
+            total = total + jnp.where(
+                slot_high == chunk, product[group * chunk:group * chunk + group], 0.0
+            )
+        for part in range(2):
+            row = 8 * lax.div(j + part, 5) + lax.rem(j + part, 5)
+            stage[pl.ds(pl.multiple_of(row * group, 8), group), :] = total[:, 128 * part:128 * part + 128]
+        row_a, cell_a = first_copy(j)
+        row_b, cell_b = first_copy(j + 1)
+        row_code = jnp.concatenate([row_a, row_b], axis=1)
+        cell_code = jnp.concatenate([cell_a, cell_b], axis=1)
+        here = row_iota((40, 256)) == slot_high
+        codes = jnp.concatenate(
+            [jnp.where(here, row_code, 0), jnp.where(here, cell_code, 0)], axis=0
+        ).astype(jnp.float32).astype(jnp.bfloat16)
+        inverse[...] += lax.dot_general(
+            codes, one_hot, (((1,), (1,)), ((), ())), preferred_element_type=jnp.float32
+        )
+        return carry
+
+    lax.fori_loop(0, HALF, step, 0)
+    for v in range(vectors + 1):
+        column = stage[pl.ds(v, ROWS, stride=group), :]
+        nodal[ROWS * v:ROWS * v + ROWS, :] = column
+        top = stage[pl.ds(4 * group + v, 25, stride=8 * group), :]
+        top_high = top.astype(jnp.bfloat16).astype(jnp.float32)
+        both = jnp.where(lane >= 64, top - top_high, pltpu.roll(top_high, 64, 1))
+        face[32 * v:32 * v + 32, :] = jnp.concatenate(
+            [both, jnp.zeros((7, 128), jnp.float32)], axis=0
+        ).astype(jnp.bfloat16)
+
+
+def shared_sums(terms):
+    lane = lane_iota((8, 128))
+    row = row_iota((8, 128))
+    cell_z, cell_x, cell_y = lane >> 6, lane >> 3 & 7, lane & 7
+    block = [terms[8 * k:8 * k + 8] for k in range(25)]
+    for b in range(5):
+        first, last = block[b], block[20 + b]
+        block[b] = first + jnp.where(cell_x > 0, pltpu.roll(last, 8, 1), 0.0)
+        block[20 + b] = last + jnp.where(cell_x < 7, pltpu.roll(first, 120, 1), 0.0)
+    for a in range(5):
+        first, last = block[5 * a], block[5 * a + 4]
+        block[5 * a] = first + jnp.where(cell_y > 0, pltpu.roll(last, 1, 1), 0.0)
+        block[5 * a + 4] = last + jnp.where(cell_y < 7, pltpu.roll(first, 127, 1), 0.0)
+    joined = ((row == 0) & (cell_z == 1)) | ((row == 4) & (cell_z == 0))
+    for k in range(25):
+        other = pltpu.roll(pltpu.roll(block[k], 64, 1), 4, 0)
+        block[k] = block[k] + jnp.where(joined, other, 0.0)
+    return jnp.concatenate(block, axis=0)
+
+
+def cell_operator(pair, stiffness, cell_data):
+    values = jnp.concatenate(pair, axis=1).astype(jnp.bfloat16)
+    stiff = jnp.dot(stiffness, values, preferred_element_type=jnp.float32)
+    coefficient, kinetic = cell_data[:ROWS], cell_data[ROWS:ROWS + 1]
+    results = []
+    for part in range(2):
+        columns = slice(128 * part, 128 * part + 128)
+        low = values[:, columns].astype(jnp.float32)
+        results.append(shared_sums(kinetic * stiff[:, columns] + coefficient * low))
+    return results
+
+
+def face_rows(sums_ref, start):
+    lane = lane_iota((1, 128))
+    bottom = sums_ref[pl.ds(start, 25, stride=8), :]
+    top = sums_ref[pl.ds(start + 4, 25, stride=8), :]
+    rows = jnp.where(lane < 64, bottom, top)
+    return jnp.concatenate([rows, jnp.zeros((7, 128), jnp.float32)], axis=0).astype(jnp.bfloat16)
+
+
+def first_kernel(nodal_in, ghost, stiffness, cell_data, nodal, sums, face):
+    lane = lane_iota((1, 128))
+    vectors = (nodal_in.shape[0] // ROWS) - 1
+    nodal[...] = nodal_in[...]
+    for v in range(vectors + 1):
+        got = ghost[32 * v:32 * v + 32, :].astype(jnp.float32)[:25]
+        value = got + pltpu.roll(got, 64, 1)
+        old = nodal[pl.ds(ROWS * v, 25, stride=8), :]
+        nodal[pl.ds(ROWS * v, 25, stride=8), :] = jnp.where(lane < 64, value, old)
+
+    def step(i, carry):
+        start = [pl.multiple_of(2 * ROWS * i, 8), pl.multiple_of(2 * ROWS * i + ROWS, 8)]
+        pair = [nodal[pl.ds(start[k], ROWS), :] for k in range(2)]
+        result = cell_operator(pair, stiffness[...], cell_data[...])
+        for k in range(2):
+            sums[pl.ds(start[k], ROWS), :] = result[k]
+        return carry
+
+    lax.fori_loop(0, vectors // 2, step, 0)
+    for v in range(vectors):
+        face[32 * v:32 * v + 32, :] = face_rows(sums, ROWS * v)
+
+
+def add_faces(sums, v, from_above, from_below):
+    lane = lane_iota((1, 128))
+    if from_above is not None:
+        got = pltpu.roll(from_above[32 * v:32 * v + 32, :].astype(jnp.float32)[:25], 64, 1)
+        sums[pl.ds(ROWS * v + 4, 25, stride=8), :] += jnp.where(lane >= 64, got, 0.0)
+    if from_below is not None:
+        got = pltpu.roll(from_below[32 * v:32 * v + 32, :].astype(jnp.float32)[:25], 64, 1)
+        sums[pl.ds(ROWS * v, 25, stride=8), :] += jnp.where(lane < 64, got, 0.0)
+
+
+def second_kernel(
+    bounds, nodal, sums_in, from_above, from_below, stiffness, cell_data, degree, sums, face, work
+):
+    vectors = (nodal.shape[0] // ROWS) - 1
+    center, halfwidth = bounds[0], bounds[1]
+    work[...] = sums_in[...]
+    for v in range(vectors):
+        add_faces(work, v, from_above, from_below)
+    mass = nodal[ROWS * vectors:ROWS * vectors + ROWS, :]
+    squared = mass * mass
+
+    def step(i, carry):
+        start = [pl.multiple_of(2 * ROWS * i, 8), pl.multiple_of(2 * ROWS * i + ROWS, 8)]
+        pair = []
+        for k in range(2):
+            here = pl.ds(start[k], ROWS)
+            pair.append((squared * work[here, :] - center * nodal[here, :]) / halfwidth)
+            degree[here, :] = pair[k]
+        result = cell_operator(pair, stiffness[...], cell_data[...])
+        for k in range(2):
+            sums[pl.ds(start[k], ROWS), :] = result[k]
+        return carry
+
+    lax.fori_loop(0, vectors // 2, step, 0)
+    for v in range(vectors):
+        face[32 * v:32 * v + 32, :] = face_rows(sums, ROWS * v)
+
+
+def last_kernel(bounds, nodal, degree, sums_in, from_above, inverse, wave, rounded, work, spread_out):
+    vectors = wave.shape[0]
+    chunks = wave.shape[1] // 256
+    center, halfwidth = bounds[0], bounds[1]
+    work[...] = sums_in[...]
+    mass = nodal[ROWS * vectors:ROWS * vectors + ROWS, :]
+    squared = mass * mass
+    unscale = 1.0 / jnp.where(mass == 0.0, 1.0, mass)
+    spread_out[125 * vectors:126 * vectors, :] = jnp.zeros((vectors, 128), jnp.float32)
+    for v in range(vectors):
+        add_faces(work, v, from_above, None)
+        here = slice(ROWS * v, ROWS * v + ROWS)
+        second = 2.0 * (squared * work[here, :] - center * degree[here, :]) / halfwidth - nodal[here, :]
+        second = second * unscale
+        for k in range(25):
+            spread_out[pl.ds(5 * k * vectors + v, 5, stride=vectors), :] = second[8 * k:8 * k + 5]
+    table = jnp.concatenate(
+        [spread_out[:HALF * vectors, :], spread_out[HALF * vectors:2 * HALF * vectors, :]], axis=1
+    ).astype(jnp.bfloat16)
+    for chunk in range(chunks):
+        columns = slice(256 * chunk, 256 * chunk + 256)
+        row_code = inverse[chunk:chunk + 1, :].astype(jnp.int32) - 1
+        cell_code = inverse[40 + chunk:41 + chunk, :].astype(jnp.int32)
+        second_half = row_code >= HALF
+        column = jnp.where(second_half, cell_code + 128, cell_code)
+        row = jnp.where(second_half, row_code - HALF, row_code)
+        one_hot = jnp.where(row_iota((256, 256)) == column, 1.0, 0.0).astype(jnp.bfloat16)
+        product = jnp.dot(table, one_hot, preferred_element_type=jnp.float32)
+        vector = wave[:, columns]
+        one = -center * vector / halfwidth
+        unused = -2.0 * center * one / halfwidth - vector
+        total = jnp.where(row_code < 0, unused, 0.0)
+        for k in range(HALF):
+            total = total + jnp.where(row == k, product[vectors * k:vectors * k + vectors], 0.0)
+        rounded[:, columns] = total.astype(jnp.bfloat16)
+
+
+def local_call(kernel, out_shape, scratch=(), smem_first=False, inputs=0):
+    specs = [pl.BlockSpec(memory_space=pltpu.VMEM)] * inputs
+    if smem_first:
+        specs[0] = pl.BlockSpec(memory_space=pltpu.SMEM)
+    return pl.pallas_call(
+        kernel,
+        out_shape=out_shape,
+        in_specs=specs,
+        out_specs=jax.tree.map(lambda _: pl.BlockSpec(memory_space=pltpu.VMEM), out_shape),
+        scratch_shapes=list(scratch),
+        compiler_params=pltpu.CompilerParams(vmem_limit_bytes=VMEM_BYTES),
+    )
+
+
 def per_device(
     wave_block,
     connectivity,
@@ -59,48 +317,75 @@
     halfwidth,
     earlier_vectors,
 ):
-    stiffness, quadrature = gll_tables()
-    stiffness_low = jnp.asarray(stiffness).astype(jnp.bfloat16)
-    quad_weights = jnp.asarray(quadrature).astype(jnp.float32)
-    columns = wave_block.shape[0]
-    owned_count = wave_block.shape[1]
-    ghost_count = send_list.shape[0]
-    cell_count = connectivity.shape[1]
+    stiffness, quadrature, spread, reorder = fixed_tables()
+    stiffness = jnp.asarray(stiffness).astype(jnp.bfloat16)
+    vectors, owned = wave_block.shape
+    nodes, cells = connectivity.shape
+    group = vectors + 8
     cell_size = jnp.exp2(-levels.astype(jnp.float32))
-    in_use = (jnp.arange(cell_count, dtype=jnp.int32) < live_cells[0]).astype(jnp.float32)
+    in_use = (jnp.arange(cells, dtype=jnp.int32) < live_cells[0]).astype(jnp.float32)
     kinetic = cell_size / 4.0 * in_use
     volume = cell_size**3 / 8.0 * in_use
-    coefficient = volume[None, :] * quad_weights[:, None] * potential
-
-    def cell_sum(extended, cells_conn, kin_part, coeff_part):
-        values = extended[:, cells_conn].astype(jnp.bfloat16)
-        stiff_part = jnp.einsum(
-            "jk,vkc->vjc", stiffness_low, values, preferred_element_type=jnp.float32
-        )
-        cell_terms = kin_part[None, None, :] * stiff_part + coeff_part[None] * values.astype(
-            jnp.float32
-        )
-        return (
-            jnp.zeros((columns, owned_count + ghost_count), jnp.float32)
-            .at[:, cells_conn]
-            .add(cell_terms)
-        )
-
-    def apply_operator(vectors):
-        scaled = vectors * mass_scale[None, :]
-        top_face = scaled[:, send_list]
-        ghosts = passed_along(top_face.astype(jnp.bfloat16), "cells", 1).astype(top_face.dtype)
-        extended = jnp.concatenate([scaled, ghosts], 1)
-        slot_sums = cell_sum(extended, connectivity, kinetic, coefficient)
-        returned = passed_along(
-            slot_sums[:, owned_count:].astype(jnp.bfloat16), "cells", -1
-        ).astype(jnp.float32)
-        summed = slot_sums[:, :owned_count].at[:, send_list].add(returned)
-        return summed * mass_scale[None, :]
-
-    degree_one = (apply_operator(wave_block) - center * wave_block) / halfwidth
-    degree_two = 2.0 * (apply_operator(degree_one) - center * degree_one) / halfwidth - wave_block
-    rounded = degree_two.astype(jnp.bfloat16)
+    coefficient = volume[None, :] * jnp.asarray(quadrature)[:, None] * potential
+    cell_data = jnp.concatenate([coefficient, kinetic[None], jnp.zeros((2, cells), jnp.float32)], 0)
+    padding = ((0, 128 - nodes), (0, 0))
+    conn_low = jnp.pad(connectivity & 255, padding).astype(jnp.bfloat16)
+    conn_high = jnp.pad(connectivity >> 8, padding, constant_values=63).astype(jnp.bfloat16)
+    f32, bf16 = jnp.float32, jnp.bfloat16
+    shape = jax.ShapeDtypeStruct
+    bounds = jnp.stack([center, halfwidth])
+
+    nodal, face, inverse, cell_data = local_call(
+        gather_kernel,
+        (
+            shape(((vectors + 1) * ROWS, 128), f32),
+            shape(((vectors + 1) * 32, 128), bf16),
+            shape((80, 256), f32),
+            shape((208, 128), f32),
+        ),
+        [
+            pltpu.VMEM((group * owned // 256, 256), f32),
+            pltpu.VMEM((128, 128), jnp.int32),
+            pltpu.VMEM((128, 128), jnp.int32),
+            pltpu.VMEM((ROWS * group + group * 8, 128), f32),
+        ],
+        inputs=7,
+    )(wave_block, mass_scale[None], conn_high, conn_low, cell_data, jnp.asarray(spread), jnp.asarray(reorder))
+    ghost = passed_along(face, "cells", 1)
+    nodal, sums, face = local_call(
+        first_kernel,
+        (
+            shape(((vectors + 1) * ROWS, 128), f32),
+            shape((vectors * ROWS, 128), f32),
+            shape((vectors * 32, 128), bf16),
+        ),
+        inputs=4,
+    )(nodal, ghost, stiffness, cell_data)
+    from_above = passed_along(face, "cells", -1)
+    from_below = passed_along(face, "cells", 1)
+    degree, sums, face = local_call(
+        second_kernel,
+        (
+            shape((vectors * ROWS, 128), f32),
+            shape((vectors * ROWS, 128), f32),
+            shape((vectors * 32, 128), bf16),
+        ),
+        [pltpu.VMEM((vectors * ROWS, 128), f32)],
+        smem_first=True,
+        inputs=7,
+    )(bounds, nodal, sums, from_above, from_below, stiffness, cell_data)
+    from_above = passed_along(face, "cells", -1)
+    rounded = local_call(
+        last_kernel,
+        shape((vectors, owned), bf16),
+        [
+            pltpu.VMEM((vectors * ROWS, 128), f32),
+            pltpu.VMEM((2 * HALF * vectors, 128), f32),
+        ],
+        smem_first=True,
+        inputs=7,
+    )(bounds, nodal, degree, sums, from_above, inverse, wave_block)
+
     quarter = lax.all_to_all(rounded, "vecs", split_axis=1, concat_axis=0, tiled=True)
     row_share = earlier_vectors.shape[0] // lax.axis_size(("cells", "vecs"))
     partial_sum = lax.dot_general(

time: 527 us -> 254 us (0.48)
  other arithmetic: 214 us -> 2.6 us
  local copies, waits for them, and re-layouts: 123 us -> 10.7 us
  Pallas kernels: 0 us -> 47.9 us
    scatter-add x4 -> x0, other arithmetic: 209 us -> none  [the longest x2 181 us: cell_sum(): return jnp.zeros((columns, owned_count + ghost_count), jnp.float32).at[:,...]
    gather x8 -> x0, local copies, waits for them, and re-layouts: 80.9 us -> none  [the longest x4 73.2 us: cell_sum(): values = extended[:, cells_conn].astype(jnp.bfloat16)]
    pallas_call x0 -> x4, Pallas kernels: none -> 47.9 us  [the longest x1 32.2 us: per_device(): local_call(gather_kernel, (shape(((vectors + 1) * ROWS, 128), f32), shape...]
    add x2 -> x0, local copies, waits for them, and re-layouts: 15.1 us -> none  [cell_sum(): kin_part[None, None, :] * stiff_part]
    slice x4 -> x0, local copies, waits for them, and re-layouts: 10.1 us -> none  [the longest x2 7.9 us: apply_operator(): summed = slot_sums[:, :owned_count].at[:, send_list].add(returned)]
    unnamed x11 -> x19, local copies, waits for them, and re-layouts: 0.73 us -> 9.8 us
    scatter-add x2 -> x0, local copies, waits for them, and re-layouts: 6.01 us -> none  [apply_operator(): summed = slot_sums[:, :owned_count].at[:, send_list].add(returned)]
  transfers between devices with their start and end apart: 5 -> 5, of which waited for: 4 -> 4; matrix products, arithmetic and copies ran while one was open for 2% -> 0% of each run, Pallas kernels for 0% -> 0%
where the time goes in v1:
time: 254 us; the launch traced here: 253 us
  waiting for transfers between devices  140 us (55%)
  Pallas kernels  47.9 us (19%)
  between operations  16.1 us (6%)
  matrix products  13.8 us (5%)
  starting transfers between devices  12.5 us (5%)
  local copies, waits for them, and re-layouts  10.7 us (4%)
  blocking collectives  8.99 us (4%)
  other arithmetic  2.6 us (1%)
    psum x1, waiting for transfers between devices, per_device(): projections = lax.psum(partial_sum, ('cells', 'vecs'))  129 us
    pallas_call x1, Pallas kernels, per_device(): local_call(gather_kernel, (shape(((vectors + 1) * ROWS, 128), f32), shape...  32.2 us
    ppermute x4, starting transfers between devices, passed_along(): lax.ppermute(value, axis, [(source, source + steps) for source in range(l...  12.4 us
    ppermute x4, waiting for transfers between devices, passed_along(): lax.ppermute(value, axis, [(source, source + steps) for source in range(l...  11.3 us
    unnamed x19, local copies, waits for them, and re-layouts  9.8 us
    all_to_all x1, blocking collectives, per_device(): lax.all_to_all(rounded, 'vecs', split_axis=1, concat_axis=0, tiled=True)  8.99 us
    dot_general x1, matrix products, per_device(): lax.dot_general(earlier_vectors, quarter, (((1,), (1,)), ((), ())), prefe...  7.41 us
    pallas_call x1, Pallas kernels, per_device(): local_call(last_kernel, shape((vectors, owned), bf16), [pltpu.VMEM((vecto...  7.18 us
  transfers between devices with their start and end apart: 5, of which 4 were waited for; matrix products, arithmetic and copies ran while one was open for 0% of the time, Pallas kernels for 0%

profile of v1, /device:TPU:0, one launch (start us, length us, event | category | flops | bytes accessed | tf_op | source)
XLA Modules:
  0.0 253.1 jit_solution(8613433700805057618)
XLA Ops:
  7.2 0.0 all-reduce.4.cloned.1.call-start
  7.9 0.9 and_convert_fusion
  8.7 0.7 compare_select_fusion.1
  9.4 0.1 pad.13.clone
  9.5 0.9 multiply_multiply_fusion
  10.4 0.1 maximum_maximum_fusion.cell_data
  10.5 0.0 copy-start.2
  10.5 1.1 copy-done.2
  11.6 0.0 copy-start.6
  11.6 0.9 copy-done.6
  12.5 0.0 copy-start.7
  12.5 0.8 copy-done.7
  13.3 0.0 copy-start.8
  13.3 0.8 copy-done.8
  14.1 32.2 %shard_map.140 = (f32[3400,128]{1,0:T(8,128)S(1)}, bf16[544,128]{1,0:T(8,128)(2,1)S(1)}, f32[80,256]{1,0:T(8,128)S(1)}, f32[208,128]{1,0:T(8,128)S(1)}) custom-call(f32[16,9216]{1,0:T(8,128)S(1)} %copy-done.2, f32[1,9216]{1,0:T(1,128)S(1)} %bitcast.22, bf16[128,128]{1,0:T(8,128)(2,1)S(1)} %pad.9.conn_high, bf16[128,128]{1,0:T(8,128)(2,1)S(1)} %pad.10.conn_low, ...), custom_call_target="tpu_custom_call" | custom-call | tf_op jit(solution)/shard_map/pallas_call | solution.py:338
  46.3 4.8 %collective-permute-start = (bf16[544,128]{1,0:T(8,128)(2,1)S(1)}, bf16[544,128]{1,0:T(8,128)(2,1)S(1)}, u32[]{:S(2)}, u32[]{:S(2)}) collective-permute-start(bf16[544,128]{1,0:T(8,128)(2,1)S(1)} %get-tuple-element.13), channel_id=1, source_target_pairs={{0,4},{4,8},{8,12},{12,16},{16,20},{20,24},{24,28},{1,5},{5,9},{9,... | collective-permute-start | bytes 417800 | tf_op jit(solution)/shard_map/ppermute | solution.py:20
  51.1 2.9 %collective-permute-done.ghost = bf16[544,128]{1,0:T(8,128)(2,1)S(1)} collective-permute-done((bf16[544,128]{1,0:T(8,128)(2,1)S(1)}, bf16[544,128]{1,0:T(8,128)(2,1)S(1)}, u32[]{:S(2)}, u32[]{:S(2)}) %collective-permute-start) | collective-permute-done | bytes 139296 | tf_op jit(solution)/shard_map/ppermute | solution.py:20
  54.1 0.0 copy-start.4
  54.1 0.9 copy-done.4
  55.0 3.4 %shard_map.141 = (f32[3400,128]{1,0:T(8,128)S(1)}, f32[3200,128]{1,0:T(8,128)S(1)}, bf16[512,128]{1,0:T(8,128)(2,1)S(1)}) custom-call(f32[3400,128]{1,0:T(8,128)S(1)} %get-tuple-element.12.nodal_in, bf16[544,128]{1,0:T(8,128)(2,1)S(1)} %collective-permute-done.ghost, bf16[200,200]{1,0:T(8,128)(2,1)S(1)} %copy-done.4, f32[208,128]{1,0:T(8,128)S(1)} %get-tuple-element.14.cell_data), custom_call_target="tpu_custom_call" | custom-call | tf_op jit(solution)/shard_map/pallas_call | solution.py:355
  58.4 0.0 copy-start
  58.4 1.2 copy-done
  59.6 1.3 collective-permute-start.1
  60.9 5.0 %collective-permute-start.2 = (bf16[512,128]{1,0:T(8,128)(2,1)S(1)}, bf16[512,128]{1,0:T(8,128)(2,1)S(1)}, u32[]{:S(2)}, u32[]{:S(2)}) collective-permute-start(bf16[512,128]{1,0:T(8,128)(2,1)S(1)} %get-tuple-element.17), channel_id=1, source_target_pairs={{0,4},{4,8},{8,12},{12,16},{16,20},{20,24},{24,28},{1,5},{5,9},{9,... | collective-permute-start | bytes 393224 | tf_op jit(solution)/shard_map/ppermute | solution.py:20
  67.2 0.1 pad_maximum_fusion.bounds
  67.3 0.0 collective-permute-done.1.from_above
  67.3 2.3 collective-permute-done.2.from_below
  69.6 0.0 copy-start.5
  69.6 0.9 copy-done.5
  70.5 5.1 %shard_map.142 = (f32[3200,128]{1,0:T(8,128)S(1)}, f32[3200,128]{1,0:T(8,128)S(1)}, bf16[512,128]{1,0:T(8,128)(2,1)S(1)}) custom-call(f32[2]{0:T(128)S(1)} %pad_maximum_fusion.bounds, f32[3400,128]{1,0:T(8,128)} %copy-done, f32[3200,128]{1,0:T(8,128)S(1)} %get-tuple-element.16.sums_in, bf16[512,128]{1,0:T(8,128)(2,1)S(1)} %collective-permute-done.1.from_above, ...), custom_call_target="tpu_custom_call" | custom-call | tf_op jit(solution)/shard_map/pallas_call | solution.py:366
  75.6 1.3 collective-permute-start.3
  76.9 6.1 %collective-permute-done.3.from_above = bf16[512,128]{1,0:T(8,128)(2,1)S(1)} collective-permute-done((bf16[512,128]{1,0:T(8,128)(2,1)S(1)}, bf16[512,128]{1,0:T(8,128)(2,1)S(1)}, u32[]{:S(2)}, u32[]{:S(2)}) %collective-permute-start.3) | collective-permute-done | bytes 131104 | tf_op jit(solution)/shard_map/ppermute | solution.py:20
  83.0 0.0 copy-start.1
  83.0 1.5 copy-done.1
  84.4 0.0 copy-start.3
  84.4 1.1 copy-done.3
  85.5 7.2 %shard_map.143 = bf16[16,9216]{1,0:T(8,128)(2,1)S(1)} custom-call(f32[2]{0:T(128)S(1)} %pad_maximum_fusion.bounds, f32[3400,128]{1,0:T(8,128)S(1)} %copy-done.1, f32[3200,128]{1,0:T(8,128)S(1)} %get-tuple-element.18.degree, f32[3200,128]{1,0:T(8,128)S(1)} %get-tuple-element.19.sums_in, bf16[512,128]{1,0:T(8,128)(2,1)S(1)} %collective-permute-done.3.from_above, ...), custom_call_target="tpu_custom_call" | custom-call | tf_op jit(solution)/shard_map/pallas_call | solution.py:378
  92.7 9.0 %all_to_all.19 = bf16[16,4,2304]{2,0,1:T(8,128)(2,1)S(1)} all-to-all(bf16[16,4,2304]{2,0,1:T(8,128)(2,1)S(1)} %bitcast.25), channel_id=1, replica_groups=mesh['cells'=8,'vecs'=4] {'vecs'}, dimensions={1} | all-to-all | bytes 589824 | tf_op jit(solution)/shard_map/all_to_all | solution.py:389
  101.7 7.4 %convolution_bitcast_fusion = f32[2048,64]{0,1:T(8,128)} fusion(bf16[64,2304]{1,0:T(8,128)(2,1)S(1)} %bitcast.23, bf16[2048,2304]{1,0:T(8,128)(2,1)} %param.22), kind=kOutput, calls=%fused_computation.1 | convolution fusion | flops 603979776 | bytes 10256384 | tf_op jit(solution)/shard_map/dot_general | solution.py:391
  109.1 0.0 all-reduce.4.cloned.1.call-update
  109.1 129.2 %all-reduce.4.cloned.1.call-done = f32[2048,64]{0,1:T(8,128)} async-done(((f32[2048,64]{0,1:T(8,128)}), f32[2048,64]{0,1:T(8,128)}) %all-reduce.4.cloned.1.call-update) | async-done | bytes 524304 | tf_op jit(solution)/shard_map/psum | solution.py:394
  238.3 0.8 constant_dynamic-slice_fusion
  239.1 0.7 copy.18
  239.8 6.4 %convolution_subtract_fusion = f32[64,2304]{1,0:T(8,128)} fusion(bf16[2048,2304]{1,0:T(8,128)(2,1)} %param.22, bf16[64,2304]{1,0:T(8,128)(2,1)S(1)} %bitcast.24, f32[2048,64]{0,1:T(8,128)} %all-reduce.4.cloned.1.call-done), kind=kOutput, calls=%fused_computation | convolution fusion | flops 604405760 | bytes 10846208 | tf_op jit(solution)/shard_map/dot_general | solution.py:395
  (4 shorter events, 0.0 us)
Async XLA Ops:
  7.2 231.2 %all-reduce.4.cloned.1.call-start = ((), (), s32[]{:S(2)}) async-start(), calls=%async_computation.1 | async-start | bytes 1048576 | tf_op jit(solution)/shard_map/psum | solution.py:394
  10.5 1.1 copy-start.2
  11.6 0.9 copy-start.6
  12.5 0.8 copy-start.7
  13.3 0.8 copy-start.8
  46.3 7.8 %collective-permute-start = (bf16[544,128]{1,0:T(8,128)(2,1)S(1)}, bf16[544,128]{1,0:T(8,128)(2,1)S(1)}, u32[]{:S(2)}, u32[]{:S(2)}) collective-permute-start(bf16[544,128]{1,0:T(8,128)(2,1)S(1)} %get-tuple-element.13), channel_id=1, source_target_pairs={{0,4},{4,8},{8,12},{12,16},{16,20},{20,24},{24,28},{1,5},{5,9},{9,... | collective-permute-start | bytes 417800 | tf_op jit(solution)/shard_map/ppermute | solution.py:20
  54.1 0.9 copy-start.4
  58.4 1.2 copy-start
  59.6 7.7 %collective-permute-start.1 = (bf16[512,128]{1,0:T(8,128)(2,1)S(1)}, bf16[512,128]{1,0:T(8,128)(2,1)S(1)}, u32[]{:S(2)}, u32[]{:S(2)}) collective-permute-start(bf16[512,128]{1,0:T(8,128)(2,1)S(1)} %get-tuple-element.17), channel_id=1, source_target_pairs={{4,0},{8,4},{12,8},{16,12},{20,16},{24,20},{28,24},{5,1},{9,5},{13... | collective-permute-start | bytes 393224 | tf_op jit(solution)/shard_map/ppermute | solution.py:20
  60.9 8.7 %collective-permute-start.2 = (bf16[512,128]{1,0:T(8,128)(2,1)S(1)}, bf16[512,128]{1,0:T(8,128)(2,1)S(1)}, u32[]{:S(2)}, u32[]{:S(2)}) collective-permute-start(bf16[512,128]{1,0:T(8,128)(2,1)S(1)} %get-tuple-element.17), channel_id=1, source_target_pairs={{0,4},{4,8},{8,12},{12,16},{16,20},{20,24},{24,28},{1,5},{5,9},{9,... | collective-permute-start | bytes 393224 | tf_op jit(solution)/shard_map/ppermute | solution.py:20
  69.6 0.9 copy-start.5
  75.6 7.4 %collective-permute-start.3 = (bf16[512,128]{1,0:T(8,128)(2,1)S(1)}, bf16[512,128]{1,0:T(8,128)(2,1)S(1)}, u32[]{:S(2)}, u32[]{:S(2)}) collective-permute-start(bf16[512,128]{1,0:T(8,128)(2,1)S(1)} %get-tuple-element.20), channel_id=1, source_target_pairs={{4,0},{8,4},{12,8},{16,12},{20,16},{24,20},{28,24},{5,1},{9,5},{13... | collective-permute-start | bytes 393224 | tf_op jit(solution)/shard_map/ppermute | solution.py:20
  83.0 1.5 copy-start.1
  84.4 1.1 copy-start.3
Sparse Core Ops, SparseCore 0:
  109.2 129.0 all-reduce.3

commit v2 on v1

--- a/solution.py
+++ b/solution.py
@@ -10,7 +10,7 @@
 from jax.sharding import PartitionSpec as P
 
 ROWS = 200
-HALF = 63
+GATHERED = 72
 VMEM_BYTES = 48 * 1024 * 1024
 
 
@@ -78,6 +78,45 @@
     return lax.broadcasted_iota(jnp.int32, shape, 0)
 
 
+def blocks_of(value):
+    return [value[8 * k:8 * k + 8] for k in range(value.shape[0] // 8)]
+
+
+def pack_edges(block, nothing):
+    lane = lane_iota((8, 128))
+    cell_x, cell_y = lane >> 3 & 7, lane & 7
+    edge_x = jnp.full((8, 128), nothing, block[0].dtype)
+    edge_y = edge_x
+    for b in range(4):
+        edge_x = jnp.where(cell_x == b, pltpu.roll(block[20 + b], 128 - 8 * (7 - b), 1), edge_x)
+    corner = (cell_x == 4) & (cell_y == 7)
+    edge_x = jnp.where(corner, pltpu.roll(block[24], 128 - 24, 1), edge_x)
+    for a in range(4):
+        edge_y = jnp.where(cell_y == a, pltpu.roll(block[5 * a + 4], 128 - (7 - a), 1), edge_y)
+    return edge_x, edge_y
+
+
+def fill_copies(block):
+    lane = lane_iota((8, 128))
+    row = row_iota((8, 128))
+    cell_z, cell_x, cell_y = lane >> 6, lane >> 3 & 7, lane & 7
+    edge_x, edge_y = block[25], block[26]
+    block = block[:25]
+    for b in range(4):
+        last = pltpu.roll(edge_x, 8 * (7 - b), 1) if b < 7 else edge_x
+        block[20 + b] = jnp.where(cell_x < 7, pltpu.roll(block[b], 120, 1), last)
+    for a in range(4):
+        last = pltpu.roll(edge_y, 7 - a, 1)
+        block[5 * a + 4] = jnp.where(cell_y < 7, pltpu.roll(block[5 * a], 127, 1), last)
+    last = jnp.where(cell_y < 7, pltpu.roll(block[20], 127, 1), pltpu.roll(edge_x, 24, 1))
+    block[24] = jnp.where(cell_x < 7, pltpu.roll(block[4], 120, 1), last)
+    joined = (row == 0) & (cell_z == 1)
+    for k in range(25):
+        other = pltpu.roll(pltpu.roll(block[k], 64, 1), 4, 0)
+        block[k] = jnp.where(joined, other, block[k])
+    return jnp.concatenate(block, axis=0)
+
+
 def gather_kernel(
     wave, mass, conn_high, conn_low, cell_data, spread, reorder,
     nodal, face, inverse, cell_out, packed, low, high, stage,
@@ -87,8 +126,15 @@
     group = vectors + 8
     order = reorder[...]
     order_low = order.astype(jnp.bfloat16)
-    high[...] = jnp.dot(conn_high[...], order_low, preferred_element_type=jnp.float32).astype(jnp.int32)
-    low[...] = jnp.dot(conn_low[...], order_low, preferred_element_type=jnp.float32).astype(jnp.int32)
+    spread_low = spread[:ROWS, :].astype(jnp.bfloat16)
+    for source, target, nothing in ((conn_high, high, 63), (conn_low, low, 0)):
+        spaced = jnp.dot(spread_low, source[...], preferred_element_type=jnp.float32)
+        ordered = jnp.dot(spaced.astype(jnp.bfloat16), order_low, preferred_element_type=jnp.float32)
+        ordered = ordered.astype(jnp.int32)
+        target[:ROWS, :] = ordered
+        edge_x, edge_y = pack_edges(blocks_of(ordered), nothing)
+        target[ROWS:ROWS + 8, :] = edge_x
+        target[ROWS + 8:ROWS + 16, :] = edge_y
     exact = lax.Precision.HIGHEST
     ordered = jnp.dot(cell_data[...], order, precision=exact, preferred_element_type=jnp.float32)
     cell_out[...] = jnp.dot(spread[...], ordered, precision=exact, preferred_element_type=jnp.float32)
@@ -100,38 +146,31 @@
     value = packed[...]
     value_high = value.astype(jnp.bfloat16)
     value_low = (value - value_high.astype(jnp.float32)).astype(jnp.bfloat16)
+    both = jnp.concatenate([value_high, value_low], axis=1)
     stage[...] = jnp.zeros_like(stage)
     inverse[...] = jnp.zeros_like(inverse)
     lane = lane_iota((1, 128))
-    cell_z, cell_x, cell_y = lane >> 6, lane >> 3 & 7, lane & 7
-
-    def first_copy(j):
-        a, b, c = lax.div(j, 25), lax.rem(lax.div(j, 5), 5), lax.rem(j, 5)
-        keep_x = cell_x + jnp.where(a < 4, 7, 0) >= 7
-        keep_y = cell_y + jnp.where(b < 4, 7, 0) >= 7
-        keep_z = cell_z + jnp.where(c < 4, 1, 0) >= 1
-        kept = jnp.where(keep_x & keep_y & keep_z, 1, 0)
-        return kept * (j + 1), kept * lane
+    pair_lane = lane_iota((1, 256))
 
     def step(i, carry):
-        j = 2 * i
-        slot_low = jnp.concatenate([low[pl.ds(j, 1), :], low[pl.ds(j + 1, 1), :]], axis=1)
-        slot_high = jnp.concatenate([high[pl.ds(j, 1), :], high[pl.ds(j + 1, 1), :]], axis=1)
+        at = lax.div(i, 2)
+        block = jnp.where(at < 16, 5 * lax.div(at, 4) + lax.rem(at, 4), at + 9)
+        row = 8 * block + 1 + 2 * lax.rem(i, 2)
+        slot_low = jnp.concatenate([low[pl.ds(row, 1), :], low[pl.ds(row + 1, 1), :]], axis=1)
+        slot_high = jnp.concatenate([high[pl.ds(row, 1), :], high[pl.ds(row + 1, 1), :]], axis=1)
         one_hot = jnp.where(row_iota((256, 256)) == slot_low, 1.0, 0.0).astype(jnp.bfloat16)
-        product = jnp.dot(value_high, one_hot, preferred_element_type=jnp.float32)
-        product = product + jnp.dot(value_low, one_hot, preferred_element_type=jnp.float32)
+        twice = jnp.concatenate([one_hot, one_hot], axis=0)
+        product = jnp.dot(both, twice, preferred_element_type=jnp.float32)
         total = jnp.zeros((group, 256), jnp.float32)
         for chunk in range(chunks):
             total = total + jnp.where(
                 slot_high == chunk, product[group * chunk:group * chunk + group], 0.0
             )
         for part in range(2):
-            row = 8 * lax.div(j + part, 5) + lax.rem(j + part, 5)
-            stage[pl.ds(pl.multiple_of(row * group, 8), group), :] = total[:, 128 * part:128 * part + 128]
-        row_a, cell_a = first_copy(j)
-        row_b, cell_b = first_copy(j + 1)
-        row_code = jnp.concatenate([row_a, row_b], axis=1)
-        cell_code = jnp.concatenate([cell_a, cell_b], axis=1)
+            start = pl.multiple_of((row + part) * group, 8)
+            stage[pl.ds(start, group), :] = total[:, 128 * part:128 * part + 128]
+        row_code = 2 * i + 1 + (pair_lane >> 7)
+        cell_code = pair_lane & 127
         here = row_iota((40, 256)) == slot_high
         codes = jnp.concatenate(
             [jnp.where(here, row_code, 0), jnp.where(here, cell_code, 0)], axis=0
@@ -141,15 +180,15 @@
         )
         return carry
 
-    lax.fori_loop(0, HALF, step, 0)
+    lax.fori_loop(0, GATHERED // 2, step, 0)
     for v in range(vectors + 1):
-        column = stage[pl.ds(v, ROWS, stride=group), :]
+        column = fill_copies(blocks_of(stage[pl.ds(v, ROWS + 16, stride=group), :]))
         nodal[ROWS * v:ROWS * v + ROWS, :] = column
-        top = stage[pl.ds(4 * group + v, 25, stride=8 * group), :]
+        top = nodal[pl.ds(ROWS * v + 4, 25, stride=8), :]
         top_high = top.astype(jnp.bfloat16).astype(jnp.float32)
-        both = jnp.where(lane >= 64, top - top_high, pltpu.roll(top_high, 64, 1))
+        parts = jnp.where(lane >= 64, top - top_high, pltpu.roll(top_high, 64, 1))
         face[32 * v:32 * v + 32, :] = jnp.concatenate(
-            [both, jnp.zeros((7, 128), jnp.float32)], axis=0
+            [parts, jnp.zeros((7, 128), jnp.float32)], axis=0
         ).astype(jnp.bfloat16)
 
 
@@ -262,33 +301,174 @@
     mass = nodal[ROWS * vectors:ROWS * vectors + ROWS, :]
     squared = mass * mass
     unscale = 1.0 / jnp.where(mass == 0.0, 1.0, mass)
-    spread_out[125 * vectors:126 * vectors, :] = jnp.zeros((vectors, 128), jnp.float32)
     for v in range(vectors):
         add_faces(work, v, from_above, None)
         here = slice(ROWS * v, ROWS * v + ROWS)
         second = 2.0 * (squared * work[here, :] - center * degree[here, :]) / halfwidth - nodal[here, :]
-        second = second * unscale
-        for k in range(25):
-            spread_out[pl.ds(5 * k * vectors + v, 5, stride=vectors), :] = second[8 * k:8 * k + 5]
+        block = blocks_of(second * unscale)
+        kept = [block[5 * a + b] for a in range(4) for b in range(4)]
+        for k, part in enumerate(kept + list(pack_edges(block, 0.0))):
+            spread_out[pl.ds(4 * k * vectors + v, 4, stride=vectors), :] = part[1:5]
+    middle = GATHERED // 2 * vectors
     table = jnp.concatenate(
-        [spread_out[:HALF * vectors, :], spread_out[HALF * vectors:2 * HALF * vectors, :]], axis=1
+        [spread_out[:middle, :], spread_out[middle:2 * middle, :]], axis=1
     ).astype(jnp.bfloat16)
     for chunk in range(chunks):
         columns = slice(256 * chunk, 256 * chunk + 256)
         row_code = inverse[chunk:chunk + 1, :].astype(jnp.int32) - 1
         cell_code = inverse[40 + chunk:41 + chunk, :].astype(jnp.int32)
-        second_half = row_code >= HALF
+        second_half = row_code >= GATHERED // 2
         column = jnp.where(second_half, cell_code + 128, cell_code)
-        row = jnp.where(second_half, row_code - HALF, row_code)
+        row = jnp.where(second_half, row_code - GATHERED // 2, row_code)
         one_hot = jnp.where(row_iota((256, 256)) == column, 1.0, 0.0).astype(jnp.bfloat16)
         product = jnp.dot(table, one_hot, preferred_element_type=jnp.float32)
         vector = wave[:, columns]
         one = -center * vector / halfwidth
         unused = -2.0 * center * one / halfwidth - vector
         total = jnp.where(row_code < 0, unused, 0.0)
-        for k in range(HALF):
+        for k in range(GATHERED // 2):
             total = total + jnp.where(row == k, product[vectors * k:vectors * k + vectors], 0.0)
         rounded[:, columns] = total.astype(jnp.bfloat16)
+
+
+def mesh_id(peer, others):
+    return (lax.div(peer, others), lax.rem(peer, others))
+
+
+def meet_all(me, count, others):
+    barrier = pltpu.get_barrier_semaphore()
+
+    def greet(k, carry):
+        peer = lax.rem(me + k, count)
+        pl.semaphore_signal(
+            barrier, inc=1, device_id=mesh_id(peer, others), device_id_type=pl.DeviceIdType.MESH
+        )
+        return carry
+
+    lax.fori_loop(1, count, greet, 0)
+    pl.semaphore_wait(barrier, count - 1)
+
+
+def wait_bytes(ref, semaphore):
+    pltpu.make_async_copy(ref, ref, semaphore).wait()
+
+
+def projection_kernel(
+    rows_of, others, rounded, earlier, filtered, own_rows,
+    held, quarter, partial, to_send, received, own_low, gathered, low_rows,
+    load_sem, swap_send, swap_recv, sum_send, sum_recv, all_send, all_recv,
+):
+    count = rows_of * others
+    mine, along = lax.axis_index("vecs"), lax.axis_index("cells")
+    me = along * others + mine
+    vectors = rounded.shape[0]
+    width = earlier.shape[1]
+    share = earlier.shape[0] // count
+    half = share // 2
+    parts = load_sem.shape[0]
+    depth = earlier.shape[0] // parts
+    blocks = depth // share
+    first_part = lax.div(along * parts, rows_of) + 1
+    columns = others * vectors
+    loads = []
+    for k in range(parts):
+        here = pl.ds(pl.multiple_of(lax.rem(first_part + k, parts) * depth, depth), depth)
+        loads.append(pltpu.make_async_copy(earlier.at[here], held.at[here], load_sem.at[k]))
+        loads[k].start()
+    meet_all(me, count, others)
+    for k in range(1, others):
+        peer = lax.rem(mine + k, others)
+        source = rounded.at[:, pl.ds(pl.multiple_of(peer * width, 128), width)]
+        pltpu.make_async_remote_copy(
+            source, quarter.at[mine], swap_send, swap_recv,
+            device_id=(along, peer), device_id_type=pl.DeviceIdType.MESH,
+        ).start()
+    quarter[mine] = rounded[:, pl.ds(pl.multiple_of(mine * width, 128), width)]
+    wait_bytes(quarter.at[pl.ds(0, others - 1)], swap_recv)
+    vectors_here = quarter[...].reshape(columns, width)
+    for k in range(parts):
+        part = lax.rem(first_part + k, parts)
+        loads[k].wait()
+        result = lax.dot_general(
+            held[pl.ds(pl.multiple_of(part * depth, depth), depth), :], vectors_here,
+            (((1,), (1,)), ((), ())), preferred_element_type=jnp.float32,
+        )
+        for t in range(blocks):
+            piece = result[share * t:share * t + share]
+            piece = jnp.concatenate([piece[:half], piece[half:]], axis=1)
+            partial[part * blocks + t] = piece
+            to_send[part * blocks + t] = piece.astype(jnp.bfloat16)
+        for t in range(blocks):
+            owner = part * blocks + lax.rem(me + t, blocks)
+            slot = lax.rem(owner - me + count, count) - 1
+
+            @pl.when(owner != me)
+            def _():
+                pltpu.make_async_remote_copy(
+                    to_send.at[owner], received.at[slot], sum_send, sum_recv,
+                    device_id=mesh_id(owner, others), device_id_type=pl.DeviceIdType.MESH,
+                ).start()
+
+    wait_bytes(received, sum_recv)
+    total = partial[me]
+    for k in range(count - 1):
+        total = total + received[k].astype(jnp.float32)
+    own_rows[...] = jnp.concatenate([total[:, :columns], total[:, columns:]], axis=0)
+    own_low[...] = total.astype(jnp.bfloat16)
+    gathered[me] = own_low[...]
+    for k in range(1, count):
+        peer = lax.rem(me + k, count)
+        pltpu.make_async_remote_copy(
+            own_low, gathered.at[me], all_send, all_recv,
+            device_id=mesh_id(peer, others), device_id_type=pl.DeviceIdType.MESH,
+        ).start()
+    wait_bytes(gathered.at[pl.ds(0, count - 1)], all_recv)
+    for k in range(count):
+        piece = gathered[k]
+        low_rows[share * k:share * k + half, :] = piece[:, :columns]
+        low_rows[share * k + half:share * k + share, :] = piece[:, columns:]
+    weights = low_rows[...].astype(jnp.float32).T.astype(jnp.bfloat16)
+    step = 256
+    for start in range(0, width, step):
+        here = slice(start, start + step)
+        taken = jnp.dot(weights, held[:, here], preferred_element_type=jnp.float32)
+        filtered[:, here] = vectors_here[:, here].astype(jnp.float32) - taken
+    wait_bytes(quarter.at[pl.ds(0, others - 1)], swap_send)
+    wait_bytes(received, sum_send)
+    wait_bytes(gathered.at[pl.ds(0, count - 1)], all_send)
+
+
+def project_out(rounded, earlier_vectors):
+    along, others = lax.axis_size("cells"), lax.axis_size("vecs")
+    count = along * others
+    vectors = rounded.shape[0]
+    depth, width = earlier_vectors.shape
+    share, columns = depth // count, vectors * others
+    bf16, f32 = jnp.bfloat16, jnp.float32
+    dma = pltpu.SemaphoreType.DMA
+    return pl.pallas_call(
+        functools.partial(projection_kernel, along, others),
+        out_shape=(
+            jax.ShapeDtypeStruct((columns, width), f32),
+            jax.ShapeDtypeStruct((share, columns), f32),
+        ),
+        in_specs=[pl.BlockSpec(memory_space=pltpu.VMEM), pl.BlockSpec(memory_space=pl.ANY)],
+        out_specs=(pl.BlockSpec(memory_space=pltpu.VMEM),) * 2,
+        scratch_shapes=[
+            pltpu.VMEM((depth, width), bf16),
+            pltpu.VMEM((others, vectors, width), bf16),
+            pltpu.VMEM((count, share // 2, 2 * columns), f32),
+            pltpu.VMEM((count, share // 2, 2 * columns), bf16),
+            pltpu.VMEM((count - 1, share // 2, 2 * columns), bf16),
+            pltpu.VMEM((share // 2, 2 * columns), bf16),
+            pltpu.VMEM((count, share // 2, 2 * columns), bf16),
+            pltpu.VMEM((depth, columns), bf16),
+            dma((4,)), dma, dma, dma, dma, dma, dma,
+        ],
+        compiler_params=pltpu.CompilerParams(
+            collective_id=0, has_side_effects=True, vmem_limit_bytes=VMEM_BYTES
+        ),
+    )(rounded, earlier_vectors)
 
 
 def local_call(kernel, out_shape, scratch=(), smem_first=False, inputs=0):
@@ -345,9 +525,9 @@
         ),
         [
             pltpu.VMEM((group * owned // 256, 256), f32),
-            pltpu.VMEM((128, 128), jnp.int32),
-            pltpu.VMEM((128, 128), jnp.int32),
-            pltpu.VMEM((ROWS * group + group * 8, 128), f32),
+            pltpu.VMEM((ROWS + 16, 128), jnp.int32),
+            pltpu.VMEM((ROWS + 16, 128), jnp.int32),
+            pltpu.VMEM(((ROWS + 16) * group, 128), f32),
         ],
         inputs=7,
     )(wave_block, mass_scale[None], conn_high, conn_low, cell_data, jnp.asarray(spread), jnp.asarray(reorder))
@@ -380,12 +560,15 @@
         shape((vectors, owned), bf16),
         [
             pltpu.VMEM((vectors * ROWS, 128), f32),
-            pltpu.VMEM((2 * HALF * vectors, 128), f32),
+            pltpu.VMEM((GATHERED * vectors, 128), f32),
         ],
         smem_first=True,
         inputs=7,
     )(bounds, nodal, degree, sums, from_above, inverse, wave_block)
 
+    share = earlier_vectors.shape[0] // lax.axis_size(("cells", "vecs"))
+    if share % 32 == 0:
+        return project_out(rounded, earlier_vectors)
     quarter = lax.all_to_all(rounded, "vecs", split_axis=1, concat_axis=0, tiled=True)
     row_share = earlier_vectors.shape[0] // lax.axis_size(("cells", "vecs"))
     partial_sum = lax.dot_general(

time: 254 us -> 102 us (0.40)
  waiting for transfers between devices: 140 us -> 13.8 us
  Pallas kernels: 47.9 us -> 62.3 us
  matrix products: 13.8 us -> 0 us
  between operations: 16.1 us -> 2.72 us
  blocking collectives: 8.99 us -> 0 us
  local copies, waits for them, and re-layouts: 10.7 us -> 7.21 us
    psum x1 -> x0, waiting for transfers between devices: 129 us -> none  [per_device(): projections = lax.psum(partial_sum, ('cells', 'vecs'))]
    pallas_call x0 -> x1, Pallas kernels: none -> 27.1 us  [project_out(): pl.pallas_call(functools.partial(projection_kernel, along, others), out_s...]
    dot_general x2 -> x0, matrix products: 13.8 us -> none  [the longest x1 7.41 us: per_device(): lax.dot_general(earlier_vectors, quarter, (((1,), (1,)), ((), ())), prefe...]
    pallas_call x1, Pallas kernels: 32.2 us -> 21.5 us  [per_device(): local_call(gather_kernel, (shape(((vectors + 1) * ROWS, 128), f32), shape...]
    all_to_all x1 -> x0, blocking collectives: 8.99 us -> none  [per_device(): lax.all_to_all(rounded, 'vecs', split_axis=1, concat_axis=0, tiled=True)]
    unnamed x19 -> x20, local copies, waits for them, and re-layouts: 9.8 us -> 7.12 us
  transfers between devices with their start and end apart: 5 -> 4, of which waited for: 4 -> 3; matrix products, arithmetic and copies ran while one was open for 0% -> 0% of each run, Pallas kernels for 0% -> 0%
where the time goes in v2:
time: 102 us; the launch traced here: 101 us
  Pallas kernels  62.3 us (61%)
  waiting for transfers between devices  13.8 us (14%)
  starting transfers between devices  12 us (12%)
  local copies, waits for them, and re-layouts  7.21 us (7%)
  between operations  2.72 us (3%)
  other arithmetic  2.6 us (3%)
    pallas_call x1, Pallas kernels, project_out(): pl.pallas_call(functools.partial(projection_kernel, along, others), out_s...  27.1 us
    pallas_call x1, Pallas kernels, per_device(): local_call(gather_kernel, (shape(((vectors + 1) * ROWS, 128), f32), shape...  21.5 us
    ppermute x4, waiting for transfers between devices, passed_along(): lax.ppermute(value, axis, [(source, source + steps) for source in range(l...  13.8 us
    ppermute x4, starting transfers between devices, passed_along(): lax.ppermute(value, axis, [(source, source + steps) for source in range(l...  12 us
    unnamed x20, local copies, waits for them, and re-layouts  7.12 us
    pallas_call x1, Pallas kernels, per_device(): local_call(second_kernel, (shape((vectors * ROWS, 128), f32), shape((vect...  5.24 us
    pallas_call x1, Pallas kernels, per_device(): local_call(last_kernel, shape((vectors, owned), bf16), [pltpu.VMEM((vecto...  4.98 us
    pallas_call x1, Pallas kernels, per_device(): local_call(first_kernel, (shape(((vectors + 1) * ROWS, 128), f32), shape(...  3.43 us
  transfers between devices with their start and end apart: 4, of which 3 were waited for; matrix products, arithmetic and copies ran while one was open for 0% of the time, Pallas kernels for 0%

profile of v2, /device:TPU:0, one launch (start us, length us, event | category | flops | bytes accessed | tf_op | source)
XLA Modules:
  0.0 100.6 jit_solution(7550942130725029323)
XLA Ops:
  1.3 0.9 and_convert_fusion
  2.1 0.0 copy-start.5
  2.2 0.1 pad.13.clone
  2.2 0.7 compare_select_fusion.1
  2.9 0.9 multiply_multiply_fusion
  3.9 0.1 maximum_maximum_fusion.cell_data
  3.9 0.0 copy-start.2
  4.0 1.1 %copy-done.2 = f32[16,9216]{1,0:T(8,128)S(1)} copy-done((f32[16,9216]{1,0:T(8,128)S(1)}, f32[16,9216]{1,0:T(8,128)}, u32[]{:S(2)}) %copy-start.2) | copy-done | bytes 589848
  5.0 0.0 copy-start.6
  5.0 0.9 copy-done.6
  5.9 0.0 copy-start.7
  5.9 0.8 copy-done.7
  6.8 0.0 copy-start.8
  6.8 0.8 copy-done.8
  7.5 21.5 %shard_map.140 = (f32[3400,128]{1,0:T(8,128)S(1)}, bf16[544,128]{1,0:T(8,128)(2,1)S(1)}, f32[80,256]{1,0:T(8,128)S(1)}, f32[208,128]{1,0:T(8,128)S(1)}) custom-call(f32[16,9216]{1,0:T(8,128)S(1)} %copy-done.2, f32[1,9216]{1,0:T(1,128)S(1)} %bitcast.9, bf16[128,128]{1,0:T(8,128)(2,1)S(1)} %pad.9.conn_high, bf16[128,128]{1,0:T(8,128)(2,1)S(1)} %pad.10.conn_low, ...), custom_call_target="tpu_custom_call" | custom-call | tf_op jit(solution)/shard_map/pallas_call | solution.py:518
  29.1 4.8 %collective-permute-start = (bf16[544,128]{1,0:T(8,128)(2,1)S(1)}, bf16[544,128]{1,0:T(8,128)(2,1)S(1)}, u32[]{:S(2)}, u32[]{:S(2)}) collective-permute-start(bf16[544,128]{1,0:T(8,128)(2,1)S(1)} %get-tuple-element.13), channel_id=1, source_target_pairs={{0,4},{4,8},{8,12},{12,16},{16,20},{20,24},{24,28},{1,5},{5,9},{9,... | collective-permute-start | bytes 417800 | tf_op jit(solution)/shard_map/ppermute | solution.py:20
  33.9 2.9 %collective-permute-done.ghost = bf16[544,128]{1,0:T(8,128)(2,1)S(1)} collective-permute-done((bf16[544,128]{1,0:T(8,128)(2,1)S(1)}, bf16[544,128]{1,0:T(8,128)(2,1)S(1)}, u32[]{:S(2)}, u32[]{:S(2)}) %collective-permute-start) | collective-permute-done | bytes 139296 | tf_op jit(solution)/shard_map/ppermute | solution.py:20
  36.8 0.0 copy-start.4
  36.8 0.9 copy-done.4
  37.7 3.4 %shard_map.141 = (f32[3400,128]{1,0:T(8,128)S(1)}, f32[3200,128]{1,0:T(8,128)S(1)}, bf16[512,128]{1,0:T(8,128)(2,1)S(1)}) custom-call(f32[3400,128]{1,0:T(8,128)S(1)} %get-tuple-element.12.nodal_in, bf16[544,128]{1,0:T(8,128)(2,1)S(1)} %collective-permute-done.ghost, bf16[200,200]{1,0:T(8,128)(2,1)S(1)} %copy-done.4, f32[208,128]{1,0:T(8,128)S(1)} %get-tuple-element.14.cell_data), custom_call_target="tpu_custom_call" | custom-call | tf_op jit(solution)/shard_map/pallas_call | solution.py:535
  41.2 0.0 copy-start
  41.2 1.2 %copy-done = f32[3400,128]{1,0:T(8,128)} copy-done((f32[3400,128]{1,0:T(8,128)}, f32[3400,128]{1,0:T(8,128)S(1)}, u32[]{:S(2)}) %copy-start) | copy-done | bytes 1740824
  42.4 4.4 %collective-permute-start.2 = (bf16[512,128]{1,0:T(8,128)(2,1)S(1)}, bf16[512,128]{1,0:T(8,128)(2,1)S(1)}, u32[]{:S(2)}, u32[]{:S(2)}) collective-permute-start(bf16[512,128]{1,0:T(8,128)(2,1)S(1)} %get-tuple-element.17), channel_id=1, source_target_pairs={{0,4},{4,8},{8,12},{12,16},{16,20},{20,24},{24,28},{1,5},{5,9},{9,... | collective-permute-start | bytes 393224 | tf_op jit(solution)/shard_map/ppermute | solution.py:20
  46.8 1.3 %collective-permute-start.1 = (bf16[512,128]{1,0:T(8,128)(2,1)S(1)}, bf16[512,128]{1,0:T(8,128)(2,1)S(1)}, u32[]{:S(2)}, u32[]{:S(2)}) collective-permute-start(bf16[512,128]{1,0:T(8,128)(2,1)S(1)} %get-tuple-element.17), channel_id=1, source_target_pairs={{4,0},{8,4},{12,8},{16,12},{20,16},{24,20},{28,24},{5,1},{9,5},{13... | collective-permute-start | bytes 393224 | tf_op jit(solution)/shard_map/ppermute | solution.py:20
  49.4 0.1 pad_maximum_fusion.bounds
  49.4 0.0 collective-permute-done.2.from_below
  49.5 4.6 %collective-permute-done.1.from_above = bf16[512,128]{1,0:T(8,128)(2,1)S(1)} collective-permute-done((bf16[512,128]{1,0:T(8,128)(2,1)S(1)}, bf16[512,128]{1,0:T(8,128)(2,1)S(1)}, u32[]{:S(2)}, u32[]{:S(2)}) %collective-permute-start.1) | collective-permute-done | bytes 131104 | tf_op jit(solution)/shard_map/ppermute | solution.py:20
  54.1 0.0 copy-done.5
  54.1 0.0 copy-start.1
  54.1 0.0 copy-start.3
  54.1 5.2 %shard_map.142 = (f32[3200,128]{1,0:T(8,128)S(1)}, f32[3200,128]{1,0:T(8,128)S(1)}, bf16[512,128]{1,0:T(8,128)(2,1)S(1)}) custom-call(f32[2]{0:T(128)S(1)} %pad_maximum_fusion.bounds, f32[3400,128]{1,0:T(8,128)} %copy-done, f32[3200,128]{1,0:T(8,128)S(1)} %get-tuple-element.16.sums_in, bf16[512,128]{1,0:T(8,128)(2,1)S(1)} %collective-permute-done.1.from_above, ...), custom_call_target="tpu_custom_call" | custom-call | tf_op jit(solution)/shard_map/pallas_call | solution.py:546
  59.3 1.5 %collective-permute-start.3 = (bf16[512,128]{1,0:T(8,128)(2,1)S(1)}, bf16[512,128]{1,0:T(8,128)(2,1)S(1)}, u32[]{:S(2)}, u32[]{:S(2)}) collective-permute-start(bf16[512,128]{1,0:T(8,128)(2,1)S(1)} %get-tuple-element.20), channel_id=1, source_target_pairs={{4,0},{8,4},{12,8},{16,12},{20,16},{24,20},{28,24},{5,1},{9,5},{13... | collective-permute-start | bytes 393224 | tf_op jit(solution)/shard_map/ppermute | solution.py:20
  60.8 6.3 %collective-permute-done.3.from_above = bf16[512,128]{1,0:T(8,128)(2,1)S(1)} collective-permute-done((bf16[512,128]{1,0:T(8,128)(2,1)S(1)}, bf16[512,128]{1,0:T(8,128)(2,1)S(1)}, u32[]{:S(2)}, u32[]{:S(2)}) %collective-permute-start.3) | collective-permute-done | bytes 131104 | tf_op jit(solution)/shard_map/ppermute | solution.py:20
  67.1 0.0 copy-done.1
  67.1 0.0 copy-done.3
  67.1 5.0 %shard_map.143.rounded = bf16[16,9216]{1,0:T(8,128)(2,1)S(1)} custom-call(f32[2]{0:T(128)S(1)} %pad_maximum_fusion.bounds, f32[3400,128]{1,0:T(8,128)S(1)} %copy-done.1, f32[3200,128]{1,0:T(8,128)S(1)} %get-tuple-element.18.degree, f32[3200,128]{1,0:T(8,128)S(1)} %get-tuple-element.19.sums_in, bf16[512,128]{1,0:T(8,128)(2,1)S(1)} %collective-permute-done.3.from_above, ...), custom_call_target="tpu_custom_call" | custom-call | tf_op jit(solution)/shard_map/pallas_call | solution.py:558
  72.1 27.1 %shard_map.144 = (f32[64,2304]{1,0:T(8,128)S(1)}, f32[64,64]{1,0:T(8,128)S(1)}) custom-call(bf16[16,9216]{1,0:T(8,128)(2,1)S(1)} %shard_map.143.rounded, bf16[2048,2304]{1,0:T(8,128)(2,1)} %earlier.1), custom_call_target="tpu_custom_call" | custom-call | tf_op jit(solution)/shard_map/pallas_call | solution.py:449
  99.2 0.8 copy.20
  100.0 0.6 copy.21
  (3 shorter events, 0.0 us)
Async XLA Ops:
  2.1 51.9 %copy-start.5 = (bf16[200,200]{1,0:T(8,128)(2,1)S(1)}, bf16[200,200]{1,0:T(8,128)(2,1)}, u32[]{:S(2)}) copy-start(bf16[200,200]{1,0:T(8,128)(2,1)} %constant.39.stiffness) | copy-start | bytes 240004
  3.9 1.1 %copy-start.2 = (f32[16,9216]{1,0:T(8,128)S(1)}, f32[16,9216]{1,0:T(8,128)}, u32[]{:S(2)}) copy-start(f32[16,9216]{1,0:T(8,128)} %wave.3) | copy-start | bytes 1769476
  5.0 0.9 copy-start.6
  5.9 0.8 copy-start.7
  6.8 0.8 copy-start.8
  29.1 7.8 %collective-permute-start = (bf16[544,128]{1,0:T(8,128)(2,1)S(1)}, bf16[544,128]{1,0:T(8,128)(2,1)S(1)}, u32[]{:S(2)}, u32[]{:S(2)}) collective-permute-start(bf16[544,128]{1,0:T(8,128)(2,1)S(1)} %get-tuple-element.13), channel_id=1, source_target_pairs={{0,4},{4,8},{8,12},{12,16},{16,20},{20,24},{24,28},{1,5},{5,9},{9,... | collective-permute-start | bytes 417800 | tf_op jit(solution)/shard_map/ppermute | solution.py:20
  36.8 0.9 copy-start.4
  41.2 1.2 %copy-start = (f32[3400,128]{1,0:T(8,128)}, f32[3400,128]{1,0:T(8,128)S(1)}, u32[]{:S(2)}) copy-start(f32[3400,128]{1,0:T(8,128)S(1)} %get-tuple-element.15.nodal) | copy-start | bytes 5222404
  42.4 7.1 %collective-permute-start.2 = (bf16[512,128]{1,0:T(8,128)(2,1)S(1)}, bf16[512,128]{1,0:T(8,128)(2,1)S(1)}, u32[]{:S(2)}, u32[]{:S(2)}) collective-permute-start(bf16[512,128]{1,0:T(8,128)(2,1)S(1)} %get-tuple-element.17), channel_id=1, source_target_pairs={{0,4},{4,8},{8,12},{12,16},{16,20},{20,24},{24,28},{1,5},{5,9},{9,... | collective-permute-start | bytes 393224 | tf_op jit(solution)/shard_map/ppermute | solution.py:20
  46.8 7.3 %collective-permute-start.1 = (bf16[512,128]{1,0:T(8,128)(2,1)S(1)}, bf16[512,128]{1,0:T(8,128)(2,1)S(1)}, u32[]{:S(2)}, u32[]{:S(2)}) collective-permute-start(bf16[512,128]{1,0:T(8,128)(2,1)S(1)} %get-tuple-element.17), channel_id=1, source_target_pairs={{4,0},{8,4},{12,8},{16,12},{20,16},{24,20},{28,24},{5,1},{9,5},{13... | collective-permute-start | bytes 393224 | tf_op jit(solution)/shard_map/ppermute | solution.py:20
  54.1 13.0 %copy-start.1 = (f32[3400,128]{1,0:T(8,128)S(1)}, f32[3400,128]{1,0:T(8,128)}, u32[]{:S(2)}) copy-start(f32[3400,128]{1,0:T(8,128)} %copy-done) | copy-start | bytes 5222404
  54.1 13.0 %copy-start.3 = (f32[16,9216]{1,0:T(8,128)S(1)}, f32[16,9216]{1,0:T(8,128)}, u32[]{:S(2)}) copy-start(f32[16,9216]{1,0:T(8,128)} %wave.3) | copy-start | bytes 1769476
  59.3 7.8 %collective-permute-start.3 = (bf16[512,128]{1,0:T(8,128)(2,1)S(1)}, bf16[512,128]{1,0:T(8,128)(2,1)S(1)}, u32[]{:S(2)}, u32[]{:S(2)}) collective-permute-start(bf16[512,128]{1,0:T(8,128)(2,1)S(1)} %get-tuple-element.20), channel_id=1, source_target_pairs={{4,0},{8,4},{12,8},{16,12},{20,16},{24,20},{28,24},{5,1},{9,5},{13... | collective-permute-start | bytes 393224 | tf_op jit(solution)/shard_map/ppermute | solution.py:20

commit v3 on v2

v3 whole, which is shorter than its diff:
```python
import functools
import math

import jax
import jax.numpy as jnp
import numpy as np
from jax import lax
from jax.experimental import pallas as pl
from jax.experimental.pallas import tpu as pltpu
from jax.sharding import PartitionSpec as P

ROWS = 200
GATHERED = 72
VMEM_BYTES = 36 * 1024 * 1024


def gll_tables():
    root_value = math.sqrt(3.0 / 7.0)
    points = np.array([-1.0, -root_value, 0.0, root_value, 1.0])
    weights = np.array([0.1, 49.0 / 90.0, 32.0 / 45.0, 49.0 / 90.0, 0.1])
    barycentric = np.ones(5)
    for node_index in range(5):
        for other_node in range(5):
            if other_node != node_index:
                barycentric[node_index] = barycentric[node_index] / (
                    points[node_index] - points[other_node]
                )
    derivative = np.zeros((5, 5))
    for row_index in range(5):
        for col_index in range(5):
            if row_index != col_index:
                derivative[row_index, col_index] = (
                    barycentric[col_index]
                    / barycentric[row_index]
                    / (points[row_index] - points[col_index])
                )
        derivative[row_index, row_index] = -np.sum(derivative[row_index])
    mass_one = np.zeros((5, 5))
    for node_index in range(5):
        mass_one[node_index, node_index] = weights[node_index]
    laplace_one = derivative.T @ mass_one @ derivative
    stiffness = (
        np.kron(np.kron(laplace_one, mass_one), mass_one)
        + np.kron(np.kron(mass_one, laplace_one), mass_one)
        + np.kron(np.kron(mass_one, mass_one), laplace_one)
    )
    quadrature = np.kron(np.kron(weights, weights), weights)
    return (stiffness.astype(np.float32), quadrature.astype(np.float32))


def fixed_tables():
    stiffness, quadrature = gll_tables()
    spread = np.zeros((ROWS, 125), np.float32)
    for j in range(125):
        spread[8 * (j // 5) + j % 5, j] = 1.0
    padded = np.zeros((208, 256), np.float32)
    padded[:ROWS, :ROWS] = spread @ stiffness @ spread.T
    return padded, quadrature


def lane_iota(shape):
    return lax.broadcasted_iota(jnp.int32, shape, 1)


def row_iota(shape):
    return lax.broadcasted_iota(jnp.int32, shape, 0)


def blocks_of(value):
    return [value[8 * k:8 * k + 8] for k in range(value.shape[0] // 8)]


def pack_edges(block, nothing):
    lane = lane_iota((8, 128))
    cell_x, cell_y = lane >> 3 & 7, lane & 7
    edge_x = jnp.full((8, 128), nothing, block[0].dtype)
    edge_y = edge_x
    for b in range(4):
        edge_x = jnp.where(cell_x == b, pltpu.roll(block[20 + b], 128 - 8 * (7 - b), 1), edge_x)
    corner = (cell_x == 4) & (cell_y == 7)
    edge_x = jnp.where(corner, pltpu.roll(block[24], 128 - 24, 1), edge_x)
    for a in range(4):
        edge_y = jnp.where(cell_y == a, pltpu.roll(block[5 * a + 4], 128 - (7 - a), 1), edge_y)
    return edge_x, edge_y


def fill_copies(block):
    lane = lane_iota((8, 128))
    row = row_iota((8, 128))
    cell_z, cell_x, cell_y = lane >> 6, lane >> 3 & 7, lane & 7
    edge_x, edge_y = block[25], block[26]
    block = block[:25]
    for b in range(4):
        last = pltpu.roll(edge_x, 8 * (7 - b), 1) if b < 7 else edge_x
        block[20 + b] = jnp.where(cell_x < 7, pltpu.roll(block[b], 120, 1), last)
    for a in range(4):
        last = pltpu.roll(edge_y, 7 - a, 1)
        block[5 * a + 4] = jnp.where(cell_y < 7, pltpu.roll(block[5 * a], 127, 1), last)
    last = jnp.where(cell_y < 7, pltpu.roll(block[20], 127, 1), pltpu.roll(edge_x, 24, 1))
    block[24] = jnp.where(cell_x < 7, pltpu.roll(block[4], 120, 1), last)
    joined = (row == 0) & (cell_z == 1)
    for k in range(25):
        other = pltpu.roll(pltpu.roll(block[k], 64, 1), 4, 0)
        block[k] = jnp.where(joined, other, block[k])
    return jnp.concatenate(block, axis=0)


def cell_order():
    rank, lane = row_iota((128, 128)), lane_iota((128, 128))
    x = (rank & 1) + 2 * (rank >> 3 & 1) + 4 * (rank >> 5 & 1)
    y = (rank >> 1 & 1) + 2 * (rank >> 4 & 1) + 4 * (rank >> 6 & 1)
    return jnp.where(64 * (rank >> 2 & 1) + 8 * x + y == lane, 1.0, 0.0)


def row_spread():
    row, node = row_iota((ROWS, 125)), lane_iota((ROWS, 125))
    return jnp.where(((row & 7) < 5) & (5 * (row >> 3) + (row & 7) == node), 1.0, 0.0)


def gather_kernel(
    live, wave_in, mass_in, conn_in, potential_in, levels_in, weights_in,
    nodal, face, inverse, cell_out,
    wave, mass, conn, potential, levels, weights, packed, low, high, stage, load_sem,
):
    loads = []
    sources = (conn_in, wave_in, mass_in, potential_in, levels_in, weights_in)
    targets = (conn, wave, mass, potential, levels, weights)
    for k in range(6):
        loads.append(pltpu.make_async_copy(sources[k], targets[k], load_sem.at[k]))
        loads[k].start()
    chunks = wave.shape[1] // 256
    vectors = wave.shape[0]
    group = vectors + 8
    stage[...] = jnp.zeros_like(stage)
    order, spread = cell_order(), row_spread()
    order_low, spread_low = order.astype(jnp.bfloat16), spread.astype(jnp.bfloat16)
    f32, bf16 = jnp.float32, jnp.bfloat16
    loads[0].wait()
    slots = conn[...]
    for part, target, nothing in ((slots >> 8, high, 63), (slots & 255, low, 0)):
        part = part.astype(f32).astype(bf16)
        spaced = jnp.dot(spread_low, part, preferred_element_type=f32)
        ordered = jnp.dot(spaced.astype(bf16), order_low, preferred_element_type=f32)
        ordered = ordered.astype(jnp.int32)
        target[:ROWS, :] = ordered
        edge_x, edge_y = pack_edges(blocks_of(ordered), nothing)
        target[ROWS:ROWS + 8, :] = edge_x
        target[ROWS + 8:ROWS + 16, :] = edge_y
    loads[1].wait()
    loads[2].wait()
    for chunk in range(chunks):
        columns = slice(256 * chunk, 256 * chunk + 256)
        scale = mass[:, columns]
        packed[group * chunk:group * chunk + vectors, :] = wave[:, columns] * scale
        packed[group * chunk + vectors:group * chunk + group, :] = jnp.broadcast_to(scale, (8, 256))
    value = packed[...]
    value_high = value.astype(bf16)
    value_low = (value - value_high.astype(f32)).astype(bf16)
    both = jnp.concatenate([value_high, value_low], axis=1)
    lane = lane_iota((1, 128))
    pair_lane = lane_iota((1, 256))
    blocks = [5 * a + b for a in range(4) for b in range(4)] + [25, 26]
    found = jnp.zeros((80, 256), f32)
    chunk_of = lax.broadcasted_iota(jnp.int32, (chunks, group, 256), 0)
    for i in range(GATHERED // 2):
        row = 8 * blocks[i // 2] + 1 + 2 * (i % 2)
        slot_low = jnp.concatenate([low[row:row + 1, :], low[row + 1:row + 2, :]], axis=1)
        slot_high = jnp.concatenate([high[row:row + 1, :], high[row + 1:row + 2, :]], axis=1)
        one_hot = jnp.where(row_iota((256, 256)) == slot_low, 1.0, 0.0).astype(bf16)
        twice = jnp.concatenate([one_hot, one_hot], axis=0)
        product = jnp.dot(both, twice, preferred_element_type=f32).reshape(chunks, group, 256)
        total = jnp.sum(jnp.where(chunk_of == slot_high[None], product, 0.0), axis=0)
        for part in range(2):
            start = (row + part) * group
            stage[start:start + group, :] = total[:, 128 * part:128 * part + 128]
        row_code = 2 * i + 1 + (pair_lane >> 7)
        cell_code = pair_lane & 127
        here = row_iota((40, 256)) == slot_high
        codes = jnp.concatenate(
            [jnp.where(here, row_code, 0), jnp.where(here, cell_code, 0)], axis=0
        ).astype(f32).astype(bf16)
        found = found + lax.dot_general(
            codes, one_hot, (((1,), (1,)), ((), ())), preferred_element_type=f32
        )
    inverse[...] = found
    tops = []
    for v in range(vectors + 1):
        column = fill_copies(blocks_of(stage[pl.ds(v, ROWS + 16, stride=group), :]))
        nodal[ROWS * v:ROWS * v + ROWS, :] = column
        tops.append(nodal[pl.ds(ROWS * v + 4, 25, stride=8), :])
    blank = jnp.zeros((7, 128), f32)
    for i in range(vectors // 2):
        pair = jnp.where(lane < 64, pltpu.roll(tops[2 * i], 64, 1), tops[2 * i + 1])
        face[i] = jnp.concatenate([pair, blank], axis=0).astype(bf16)
    top_high = tops[vectors].astype(bf16).astype(f32)
    parts = jnp.where(lane >= 64, tops[vectors] - top_high, pltpu.roll(top_high, 64, 1))
    face[vectors // 2] = jnp.concatenate([parts, blank], axis=0).astype(bf16)
    for k in range(3, 6):
        loads[k].wait()
    exact = lax.Precision.HIGHEST
    size = 1.0 / jnp.left_shift(1, levels[...]).astype(f32)
    in_use = jnp.where(lane < live[0], 1.0, 0.0)
    volume = size * size * size / 8.0 * in_use
    coefficient = volume * weights[:, 0:1] * potential[...]
    coefficient = jnp.dot(coefficient, order, precision=exact, preferred_element_type=f32)
    cell_out[:ROWS, :] = jnp.dot(spread, coefficient, precision=exact, preferred_element_type=f32)
    kinetic = jnp.broadcast_to(size / 4.0 * in_use, (8, 128))
    cell_out[ROWS:ROWS + 8, :] = jnp.dot(kinetic, order, precision=exact, preferred_element_type=f32)


def shared_sums(terms):
    lane = lane_iota((8, 128))
    row = row_iota((8, 128))
    cell_z, cell_x, cell_y = lane >> 6, lane >> 3 & 7, lane & 7
    block = [terms[8 * k:8 * k + 8] for k in range(25)]
    for b in range(5):
        first, last = block[b], block[20 + b]
        block[b] = first + jnp.where(cell_x > 0, pltpu.roll(last, 8, 1), 0.0)
        block[20 + b] = last + jnp.where(cell_x < 7, pltpu.roll(first, 120, 1), 0.0)
    for a in range(5):
        first, last = block[5 * a], block[5 * a + 4]
        block[5 * a] = first + jnp.where(cell_y > 0, pltpu.roll(last, 1, 1), 0.0)
        block[5 * a + 4] = last + jnp.where(cell_y < 7, pltpu.roll(first, 127, 1), 0.0)
    joined = ((row == 0) & (cell_z == 1)) | ((row == 4) & (cell_z == 0))
    for k in range(25):
        other = pltpu.roll(pltpu.roll(block[k], 64, 1), 4, 0)
        block[k] = block[k] + jnp.where(joined, other, 0.0)
    return jnp.concatenate(block, axis=0)


def cell_operator(pair, stiffness, cell_data):
    values = jnp.concatenate(pair, axis=1).astype(jnp.bfloat16)
    stiff = jnp.dot(stiffness, values, preferred_element_type=jnp.float32)
    coefficient, kinetic = cell_data[:ROWS], cell_data[ROWS:ROWS + 1]
    results = []
    for part in range(2):
        columns = slice(128 * part, 128 * part + 128)
        low = values[:, columns].astype(jnp.float32)
        results.append(shared_sums(kinetic * stiff[:, columns] + coefficient * low))
    return results


def mesh_id(peer, others):
    return (lax.div(peer, others), lax.rem(peer, others))


def meet_all(me, count, others):
    barrier = pltpu.get_barrier_semaphore()

    def greet(k, carry):
        peer = lax.rem(me + k, count)
        pl.semaphore_signal(
            barrier, inc=1, device_id=mesh_id(peer, others), device_id_type=pl.DeviceIdType.MESH
        )
        return carry

    lax.fori_loop(1, count, greet, 0)
    pl.semaphore_wait(barrier, count - 1)


def wait_bytes(ref, semaphore):
    pltpu.make_async_copy(ref, ref, semaphore).wait()


def filter_kernel(
    rows_of, others, bounds, nodal_in, face_in, inverse_in, cell_in, stiffness_in, wave_in, earlier,
    filtered, own_rows,
    nodal, inverse, cell_data, stiffness, wave, sums, degree, edge, spread_out, rounded,
    ghost, above, below, above_again, bottoms, tops, bottoms_again,
    held, quarter, partial, to_send, received, own_low, gathered, low_rows,
    input_sem, load_sem, ghost_send, ghost_recv, up_send, up_recv, down_send, down_recv,
    again_send, again_recv, swap_send, swap_recv, sum_send, sum_recv, all_send, all_recv,
):
    count = rows_of * others
    mine, along = lax.axis_index("vecs"), lax.axis_index("cells")
    me = along * others + mine
    vectors = wave.shape[0]
    pairs = vectors // 2
    width = earlier.shape[1]
    share = earlier.shape[0] // count
    half = share // 2
    parts = load_sem.shape[0]
    depth = earlier.shape[0] // parts
    blocks = depth // share
    first_part = lax.div(along * parts, rows_of) + 1
    columns = others * vectors
    f32, bf16 = jnp.float32, jnp.bfloat16
    center, halfwidth = bounds[0], bounds[1]
    lane = lane_iota((1, 128))
    inputs = []
    sources = (nodal_in, cell_in, stiffness_in, inverse_in, wave_in)
    targets = (nodal, cell_data, stiffness, inverse, wave)
    for k in range(5):
        inputs.append(pltpu.make_async_copy(sources[k], targets[k], input_sem.at[k]))
        inputs[k].start()
    has_above, has_below = along < rows_of - 1, along > 0

    def to_neighbour(source, target, step, send, recv):
        return pltpu.make_async_remote_copy(
            source, target, send, recv,
            device_id=(along + step, mine), device_id_type=pl.DeviceIdType.MESH,
        )

    meet_all(me, count, others)

    @pl.when(has_above)
    def _():
        to_neighbour(face_in, ghost, 1, ghost_send, ghost_recv).start()

    loads = []
    for k in range(parts):
        here = pl.ds(pl.multiple_of(lax.rem(first_part + k, parts) * depth, depth), depth)
        loads.append(pltpu.make_async_copy(earlier.at[here], held.at[here], load_sem.at[k]))
        loads[k].start()

    @pl.when(jnp.logical_not(has_above))
    def _():
        above[...] = jnp.zeros_like(above)
        above_again[...] = jnp.zeros_like(above_again)

    @pl.when(jnp.logical_not(has_below))
    def _():
        below[...] = jnp.zeros_like(below)
        ghost[...] = jnp.zeros_like(ghost)

    for k in range(5):
        inputs[k].wait()

    @pl.when(has_below)
    def _():
        wait_bytes(ghost, ghost_recv)

    for v in range(vectors + 1):
        got = ghost[v // 2].astype(f32)[:25]
        turned = pltpu.roll(got, 64, 1)
        value = got + turned if v == vectors else (turned if v % 2 else got)
        here = pl.ds(ROWS * v, 25, stride=8)
        nodal[here, :] = jnp.where(lane < 64, value, nodal[here, :])
    blank = jnp.zeros((7, 128), f32)

    def bottom_faces():
        first, second = edge[pl.ds(0, 25, stride=8), :], edge[pl.ds(ROWS, 25, stride=8), :]
        rows = jnp.where(lane < 64, first, pltpu.roll(second, 64, 1))
        return jnp.concatenate([rows, blank], axis=0).astype(bf16)

    def top_faces():
        first, second = edge[pl.ds(4, 25, stride=8), :], edge[pl.ds(ROWS + 4, 25, stride=8), :]
        rows = jnp.where(lane < 64, pltpu.roll(first, 64, 1), second)
        return jnp.concatenate([rows, blank], axis=0).astype(bf16)

    def add_above(faces):
        got = faces.astype(f32)[:25]
        for k, value in enumerate((pltpu.roll(got, 64, 1), got)):
            edge[pl.ds(ROWS * k + 4, 25, stride=8), :] += jnp.where(lane >= 64, value, 0.0)

    def add_below(faces):
        got = faces.astype(f32)[:25]
        for k, value in enumerate((got, pltpu.roll(got, 64, 1))):
            edge[pl.ds(ROWS * k, 25, stride=8), :] += jnp.where(lane < 64, value, 0.0)

    def both_rows(i):
        return pl.ds(pl.multiple_of(2 * ROWS * i, 16), 2 * ROWS)

    def apply(values):
        result = cell_operator(
            [values[:ROWS], values[ROWS:]], stiffness[:ROWS, :ROWS], cell_data[...]
        )
        for k in range(2):
            edge[ROWS * k:ROWS * k + ROWS, :] = result[k]

    def first_step(i, carry):
        apply(nodal[both_rows(i), :])
        sums[both_rows(i), :] = edge[...]
        bottoms[i] = bottom_faces()
        tops[i] = top_faces()

        @pl.when(has_below)
        def _():
            to_neighbour(bottoms.at[i], above.at[i], -1, up_send, up_recv.at[i]).start()

        @pl.when(has_above)
        def _():
            to_neighbour(tops.at[i], below.at[i], 1, down_send, down_recv.at[i]).start()

        return carry

    lax.fori_loop(0, pairs, first_step, 0)
    mass = nodal[ROWS * vectors:ROWS * vectors + ROWS, :]
    squared = jnp.concatenate([mass * mass, mass * mass], axis=0)

    def second_step(i, carry):
        @pl.when(has_above)
        def _():
            wait_bytes(above.at[i], up_recv.at[i])

        @pl.when(has_below)
        def _():
            wait_bytes(below.at[i], down_recv.at[i])

        edge[...] = sums[both_rows(i), :]
        add_above(above[i])
        add_below(below[i])
        one = (squared * edge[...] - center * nodal[both_rows(i), :]) / halfwidth
        degree[both_rows(i), :] = one
        apply(one)
        sums[both_rows(i), :] = edge[...]
        bottoms_again[i] = bottom_faces()

        @pl.when(has_below)
        def _():
            to_neighbour(
                bottoms_again.at[i], above_again.at[i], -1, again_send, again_recv.at[i]
            ).start()

        return carry

    lax.fori_loop(0, pairs, second_step, 0)
    unscale = 1.0 / jnp.where(mass == 0.0, 1.0, mass)
    for i in range(pairs):
        @pl.when(has_above)
        def _():
            wait_bytes(above_again.at[i], again_recv.at[i])

        here = both_rows(i)
        edge[...] = sums[here, :]
        add_above(above_again[i])
        two = 2.0 * (squared * edge[...] - center * degree[here, :]) / halfwidth - nodal[here, :]
        for k in range(2):
            v = 2 * i + k
            block = blocks_of(two[ROWS * k:ROWS * k + ROWS] * unscale)
            kept = [block[5 * a + b] for a in range(4) for b in range(4)]
            for n, part in enumerate(kept + list(pack_edges(block, 0.0))):
                spread_out[pl.ds(4 * n * vectors + v, 4, stride=vectors), :] = part[1:5]
    middle = GATHERED // 2 * vectors
    table = jnp.concatenate(
        [spread_out[:middle, :], spread_out[middle:2 * middle, :]], axis=1
    ).astype(bf16)
    chunks = width // 256
    row_of = lax.broadcasted_iota(jnp.int32, (GATHERED // 2, vectors, 256), 0)
    for q in range(others):
        peer = lax.rem(mine + 1 + q, others)
        for k in range(chunks):
            chunk = peer * chunks + k
            row_code = inverse[pl.ds(chunk, 1), :].astype(jnp.int32) - 1
            cell_code = inverse[pl.ds(40 + chunk, 1), :].astype(jnp.int32)
            second_half = row_code >= GATHERED // 2
            column = jnp.where(second_half, cell_code + 128, cell_code)
            row = jnp.where(second_half, row_code - GATHERED // 2, row_code)
            one_hot = jnp.where(row_iota((256, 256)) == column, 1.0, 0.0).astype(bf16)
            product = jnp.dot(table, one_hot, preferred_element_type=f32)
            product = product.reshape(GATHERED // 2, vectors, 256)
            total = jnp.sum(jnp.where(row_of == row[None], product, 0.0), axis=0)
            here = pl.ds(pl.multiple_of(chunk * 256, 256), 256)
            vector = wave[:, here]
            one = -center * vector / halfwidth
            unused = -2.0 * center * one / halfwidth - vector
            rounded[:, here] = jnp.where(row_code < 0, unused, total).astype(bf16)
        source = rounded.at[:, pl.ds(pl.multiple_of(peer * width, 128), width)]
        if q < others - 1:
            pltpu.make_async_remote_copy(
                source, quarter.at[mine], swap_send, swap_recv,
                device_id=(along, peer), device_id_type=pl.DeviceIdType.MESH,
            ).start()
        else:
            quarter[mine] = source[...]
    wait_bytes(quarter.at[pl.ds(0, others - 1)], swap_recv)
    vectors_here = quarter[...].reshape(columns, width)
    for k in range(parts):
        part = lax.rem(first_part + k, parts)
        loads[k].wait()
        result = lax.dot_general(
            held[pl.ds(pl.multiple_of(part * depth, depth), depth), :], vectors_here,
            (((1,), (1,)), ((), ())), preferred_element_type=jnp.float32,
        )
        for t in range(blocks):
            piece = result[share * t:share * t + share]
            piece = jnp.concatenate([piece[:half], piece[half:]], axis=1)
            partial[part * blocks + t] = piece
            to_send[part * blocks + t] = piece.astype(jnp.bfloat16)
        for t in range(blocks):
            owner = part * blocks + lax.rem(me + t, blocks)
            slot = lax.rem(owner - me + count, count) - 1

            @pl.when(owner != me)
            def _():
                pltpu.make_async_remote_copy(
                    to_send.at[owner], received.at[slot], sum_send, sum_recv,
                    device_id=mesh_id(owner, others), device_id_type=pl.DeviceIdType.MESH,
                ).start()

    wait_bytes(received, sum_recv)
    total = partial[me]
    for k in range(count - 1):
        total = total + received[k].astype(jnp.float32)
    own_rows[...] = jnp.concatenate([total[:, :columns], total[:, columns:]], axis=0)
    own_low[...] = total.astype(jnp.bfloat16)
    gathered[me] = own_low[...]
    for k in range(1, count):
        peer = lax.rem(me + k, count)
        pltpu.make_async_remote_copy(
            own_low, gathered.at[me], all_send, all_recv,
            device_id=mesh_id(peer, others), device_id_type=pl.DeviceIdType.MESH,
        ).start()
    wait_bytes(gathered.at[pl.ds(0, count - 1)], all_recv)
    for k in range(count):
        piece = gathered[k]
        low_rows[share * k:share * k + half, :] = piece[:, :columns]
        low_rows[share * k + half:share * k + share, :] = piece[:, columns:]
    weights = low_rows[...].astype(jnp.float32).T.astype(jnp.bfloat16)
    step = 256
    for start in range(0, width, step):
        here = slice(start, start + step)
        taken = jnp.dot(weights, held[:, here], preferred_element_type=jnp.float32)
        filtered[:, here] = vectors_here[:, here].astype(jnp.float32) - taken
    wait_bytes(quarter.at[pl.ds(0, others - 1)], swap_send)
    wait_bytes(received, sum_send)
    wait_bytes(gathered.at[pl.ds(0, count - 1)], all_send)

    @pl.when(has_above)
    def _():
        wait_bytes(ghost, ghost_send)
        wait_bytes(tops, down_send)

    @pl.when(has_below)
    def _():
        wait_bytes(bottoms, up_send)
        wait_bytes(bottoms_again, again_send)


def filter_block(bounds, nodal, face, inverse, cell_data, stiffness, wave_block, earlier_vectors):
    along, others = lax.axis_size("cells"), lax.axis_size("vecs")
    count = along * others
    vectors, owned = wave_block.shape
    depth, width = earlier_vectors.shape
    share, columns = depth // count, vectors * others
    bf16, f32 = jnp.bfloat16, jnp.float32
    dma = pltpu.SemaphoreType.DMA
    pairs = vectors // 2
    faces = pltpu.VMEM((pairs, 32, 128), bf16)
    block = (share // 2, 2 * columns)
    return pl.pallas_call(
        functools.partial(filter_kernel, along, others),
        out_shape=(
            jax.ShapeDtypeStruct((columns, width), f32),
            jax.ShapeDtypeStruct((share, columns), f32),
        ),
        in_specs=[pl.BlockSpec(memory_space=pltpu.SMEM)] + [pl.BlockSpec(memory_space=pl.ANY)] * 7,
        out_specs=(pl.BlockSpec(memory_space=pltpu.VMEM),) * 2,
        scratch_shapes=[
            pltpu.VMEM(nodal.shape, f32),
            pltpu.VMEM(inverse.shape, f32),
            pltpu.VMEM(cell_data.shape, f32),
            pltpu.VMEM(stiffness.shape, bf16),
            pltpu.VMEM((vectors, owned), f32),
            pltpu.VMEM((vectors * ROWS, 128), f32),
            pltpu.VMEM((vectors * ROWS, 128), f32),
            pltpu.VMEM((2 * ROWS, 128), f32),
            pltpu.VMEM((GATHERED * vectors, 128), f32),
            pltpu.VMEM((vectors, owned), bf16),
            pltpu.VMEM((pairs + 1, 32, 128), bf16),
            faces, faces, faces, faces, faces, faces,
            pltpu.VMEM((depth, width), bf16),
            pltpu.VMEM((others, vectors, width), bf16),
            pltpu.VMEM((count,) + block, f32),
            pltpu.VMEM((count,) + block, bf16),
            pltpu.VMEM((count - 1,) + block, bf16),
            pltpu.VMEM(block, bf16),
            pltpu.VMEM((count,) + block, bf16),
            pltpu.VMEM((depth, columns), bf16),
            dma((5,)), dma((4,)), dma, dma, dma, dma((pairs,)), dma, dma((pairs,)),
            dma, dma((pairs,)), dma, dma, dma, dma, dma, dma,
        ],
        compiler_params=pltpu.CompilerParams(
            collective_id=0, has_side_effects=True, vmem_limit_bytes=VMEM_BYTES
        ),
    )(bounds, nodal, face, inverse, cell_data, stiffness, wave_block, earlier_vectors)


def per_device(
    wave_block,
    connectivity,
    send_list,
    levels,
    live_cells,
    potential,
    mass_scale,
    center,
    halfwidth,
    earlier_vectors,
):
    stiffness, quadrature = fixed_tables()
    stiffness = jnp.asarray(stiffness).astype(jnp.bfloat16)
    weights = jnp.asarray(np.broadcast_to(quadrature[:, None], (125, 128)))
    vectors, owned = wave_block.shape
    nodes, cells = connectivity.shape
    group = vectors + 8
    f32, bf16 = jnp.float32, jnp.bfloat16
    shape = jax.ShapeDtypeStruct
    whole = pl.BlockSpec(memory_space=pltpu.VMEM)
    nodal, face, inverse, cell_data = pl.pallas_call(
        gather_kernel,
        out_shape=(
            shape(((vectors + 1) * ROWS, 128), f32),
            shape((vectors // 2 + 1, 32, 128), bf16),
            shape((80, 256), f32),
            shape((208, 128), f32),
        ),
        in_specs=[pl.BlockSpec(memory_space=pltpu.SMEM)] + [pl.BlockSpec(memory_space=pl.ANY)] * 6,
        out_specs=(whole,) * 4,
        scratch_shapes=[
            pltpu.VMEM((vectors, owned), f32),
            pltpu.VMEM((1, owned), f32),
            pltpu.VMEM((nodes, cells), jnp.int32),
            pltpu.VMEM((nodes, cells), f32),
            pltpu.VMEM((1, cells), jnp.int32),
            pltpu.VMEM((nodes, 128), f32),
            pltpu.VMEM((group * owned // 256, 256), f32),
            pltpu.VMEM((ROWS + 16, 128), jnp.int32),
            pltpu.VMEM((ROWS + 16, 128), jnp.int32),
            pltpu.VMEM(((ROWS + 16) * group, 128), f32),
            pltpu.SemaphoreType.DMA((6,)),
        ],
        compiler_params=pltpu.CompilerParams(vmem_limit_bytes=VMEM_BYTES),
    )(live_cells, wave_block, mass_scale[None], connectivity, potential, levels[None], weights)
    bounds = jnp.stack([center, halfwidth])
    share = earlier_vectors.shape[0] // lax.axis_size(("cells", "vecs"))
    return filter_block(
        bounds, nodal, face, inverse, cell_data, stiffness, wave_block, earlier_vectors
    )


def solution(mesh):
    in_specs = (
        P("vecs", "cells"),
        P(None, "cells"),
        P("cells"),
        P("cells"),
        P("cells"),
        P(None, "cells"),
        P("cells"),
        P(),
        P(),
        P(None, ("cells", "vecs")),
    )
    out_specs = (P(None, ("cells", "vecs")), P(("cells", "vecs"), None))
    return jax.shard_map(
        per_device, mesh=mesh, in_specs=in_specs, out_specs=out_specs, check_vma=False
    )
```

time: 102 us -> 72.2 us (0.71)
  waiting for transfers between devices: 13.8 us -> 0 us
  starting transfers between devices: 12 us -> 0 us
  Pallas kernels: 62.3 us -> 58.2 us
  local copies, waits for them, and re-layouts: 7.21 us -> 10.9 us
  other arithmetic: 2.6 us -> 0.08 us
    ppermute x4 -> x0, waiting for transfers between devices: 13.8 us -> none  [passed_along(): lax.ppermute(value, axis, [(source, source + steps) for source in range(l...]
    ppermute x4 -> x0, starting transfers between devices: 12 us -> none  [passed_along(): lax.ppermute(value, axis, [(source, source + steps) for source in range(l...]
    pallas_call x5 -> x2, Pallas kernels: 62.3 us -> 58.2 us  [the longest x1 46.2 us: filter_block(): pl.pallas_call(functools.partial(filter_kernel, along, others), out_shape...]
    unnamed x20 -> x16, local copies, waits for them, and re-layouts: 7.12 us -> 10.2 us
    mul x2 -> x0, other arithmetic: 1.59 us -> none  [the longest x1 0.92 us: per_device(): coefficient = volume[None, :] * jnp.asarray(quadrature)[:, None] * potential]
  transfers between devices with their start and end apart: 4 -> 0, of which waited for: 3 -> 0; matrix products, arithmetic and copies ran while one was open for 0% -> 0% of each run, Pallas kernels for 0% -> 0%
where the time goes in v3:
time: 72.2 us; the launch traced here: 71.8 us
  Pallas kernels  58.2 us (81%)
  local copies, waits for them, and re-layouts  10.9 us (15%)
  between operations  2.61 us (4%)
    pallas_call x1, Pallas kernels, filter_block(): pl.pallas_call(functools.partial(filter_kernel, along, others), out_shape...  46.2 us
    pallas_call x1, Pallas kernels, per_device(): pl.pallas_call(gather_kernel, out_shape=(shape(((vectors + 1) * ROWS, 128...  12 us
    unnamed x16, local copies, waits for them, and re-layouts  10.2 us

profile of v3, /device:TPU:0, one launch (start us, length us, event | category | flops | bytes accessed | tf_op | source)
XLA Modules:
  0.0 71.8 jit_solution(12479583441694094981)
XLA Ops:
  2.6 0.1 pad_maximum_fusion.bounds
  2.6 0.7 %jit_solution_.3.weights_in = f32[125,128]{1,0:T(8,128)S(1)} broadcast(f32[125]{0:T(128)} %constant.5.clone), dimensions={0} | broadcast | bytes 64500 | tf_op jit(solution)
  3.4 0.0 copy-start.1
  3.4 1.1 %copy-done.1 = f32[16,9216]{1,0:T(8,128)S(1)} copy-done((f32[16,9216]{1,0:T(8,128)S(1)}, f32[16,9216]{1,0:T(8,128)}, u32[]{:S(2)}) %copy-start.1) | copy-done | bytes 589848
  4.4 0.0 copy-start.3
  4.4 0.8 %copy-done.3 = s32[125,128]{1,0:T(8,128)S(1)} copy-done((s32[125,128]{1,0:T(8,128)S(1)}, s32[125,128]{1,0:T(8,128)}, u32[]{:S(2)}) %copy-start.3) | copy-done | bytes 64024
  5.3 0.0 copy-start.4
  5.3 0.8 %copy-done.4 = f32[125,128]{1,0:T(8,128)S(1)} copy-done((f32[125,128]{1,0:T(8,128)S(1)}, f32[125,128]{1,0:T(8,128)}, u32[]{:S(2)}) %copy-start.4) | copy-done | bytes 64024
  6.1 0.0 copy-start.5
  6.1 0.8 %copy-done.5 = f32[9216]{0:T(1024)S(1)} copy-done((f32[9216]{0:T(1024)S(1)}, f32[9216]{0:T(1024)}, u32[]{:S(2)}) %copy-start.5) | copy-done | bytes 36888
  6.9 0.0 copy-start.6
  6.9 0.7 copy-done.6
  7.5 12.0 %shard_map.122 = (f32[3400,128]{1,0:T(8,128)S(1)}, bf16[9,32,128]{2,1,0:T(8,128)(2,1)S(1)}, f32[80,256]{1,0:T(8,128)S(1)}, f32[208,128]{1,0:T(8,128)S(1)}) custom-call(s32[1]{0:T(128)S(6)} %copy.15.live, f32[16,9216]{1,0:T(8,128)S(1)} %copy-done.1, f32[1,9216]{1,0:T(1,128)S(1)} %bitcast.6, s32[125,128]{1,0:T(8,128)S(1)} %copy-done.3, ...), custom_call_target="tpu_custom_call" | custom-call | tf_op jit(solution)/shard_map/pallas_call | solution.py:600
  19.6 0.0 copy-start
  19.6 3.7 %copy-done = bf16[2048,2304]{1,0:T(8,128)(2,1)S(1)} copy-done((bf16[2048,2304]{1,0:T(8,128)(2,1)S(1)}, bf16[2048,2304]{1,0:T(8,128)(2,1)}, u32[]{:S(2)}) %copy-start) | copy-done | bytes 9437208
  23.3 0.0 copy-start.2
  23.3 0.9 %copy-done.2 = bf16[208,256]{1,0:T(8,128)(2,1)S(1)} copy-done((bf16[208,256]{1,0:T(8,128)(2,1)S(1)}, bf16[208,256]{1,0:T(8,128)(2,1)}, u32[]{:S(2)}) %copy-start.2) | copy-done | bytes 106520
  24.2 46.2 %shard_map.123 = (f32[64,2304]{1,0:T(8,128)S(1)}, f32[64,64]{1,0:T(8,128)S(1)}) custom-call(f32[2]{0:T(128)S(1)} %pad_maximum_fusion.bounds, f32[3400,128]{1,0:T(8,128)S(1)} %get-tuple-element.6.nodal_in, bf16[9,32,128]{2,1,0:T(8,128)(2,1)S(1)} %get-tuple-element.7.face_in, f32[80,256]{1,0:T(8,128)S(1)} %get-tuple-element.8.inverse_in, ...), custom_call_target="tpu_custom_call" | custom-call | tf_op jit(solution)/shard_map/pallas_call | solution.py:541
  70.3 0.8 %copy.18 = f32[64,2304]{1,0:T(8,128)} copy(f32[64,2304]{1,0:T(8,128)S(1)} %get-tuple-element.12) | data formatting | bytes 1179648
  71.2 0.6 copy.19
Async XLA Ops:
  3.4 1.1 %copy-start.1 = (f32[16,9216]{1,0:T(8,128)S(1)}, f32[16,9216]{1,0:T(8,128)}, u32[]{:S(2)}) copy-start(f32[16,9216]{1,0:T(8,128)} %wave_in.3) | copy-start | bytes 1769476
  4.4 0.8 %copy-start.3 = (s32[125,128]{1,0:T(8,128)S(1)}, s32[125,128]{1,0:T(8,128)}, u32[]{:S(2)}) copy-start(s32[125,128]{1,0:T(8,128)} %conn_in.1) | copy-start | bytes 192004
  5.3 0.8 %copy-start.4 = (f32[125,128]{1,0:T(8,128)S(1)}, f32[125,128]{1,0:T(8,128)}, u32[]{:S(2)}) copy-start(f32[125,128]{1,0:T(8,128)} %potential_in.1) | copy-start | bytes 192004
  6.1 0.8 %copy-start.5 = (f32[9216]{0:T(1024)S(1)}, f32[9216]{0:T(1024)}, u32[]{:S(2)}) copy-start(f32[9216]{0:T(1024)} %param.17) | copy-start | bytes 110596
  6.9 0.7 copy-start.6
  19.6 3.7 %copy-start = (bf16[2048,2304]{1,0:T(8,128)(2,1)S(1)}, bf16[2048,2304]{1,0:T(8,128)(2,1)}, u32[]{:S(2)}) copy-start(bf16[2048,2304]{1,0:T(8,128)(2,1)} %earlier.1) | copy-start | bytes 28311556
  23.3 0.9 %copy-start.2 = (bf16[208,256]{1,0:T(8,128)(2,1)S(1)}, bf16[208,256]{1,0:T(8,128)(2,1)}, u32[]{:S(2)}) copy-start(bf16[208,256]{1,0:T(8,128)(2,1)} %constant.7.stiffness_in) | copy-start | bytes 319492

commit v4 on v3

--- a/solution.py
+++ b/solution.py
@@ -11,7 +11,7 @@
 
 ROWS = 200
 GATHERED = 72
-VMEM_BYTES = 36 * 1024 * 1024
+VMEM_BYTES = 60 * 1024 * 1024
 
 
 def gll_tables():
@@ -117,17 +117,20 @@
     return jnp.where(((row & 7) < 5) & (5 * (row >> 3) + (row & 7) == node), 1.0, 0.0)
 
 
-def gather_kernel(
-    live, wave_in, mass_in, conn_in, potential_in, levels_in, weights_in,
-    nodal, face, inverse, cell_out,
-    wave, mass, conn, potential, levels, weights, packed, low, high, stage, load_sem,
+def node_weights():
+    node = row_iota((125, 128))
+
+    def weight(index):
+        return jnp.where(index == 2, 32.0 / 45.0, jnp.where((index & 3) == 0, 0.1, 49.0 / 90.0))
+
+    a, ab = node * 41 >> 10, node * 205 >> 10
+    return weight(a) * weight(ab - 5 * a) * weight(node - 5 * ab)
+
+
+def gather_nodes(
+    live, wave, mass, conn, potential, levels, nodal, face, inverse, cell_out,
+    packed, low, high, stage, loads,
 ):
-    loads = []
-    sources = (conn_in, wave_in, mass_in, potential_in, levels_in, weights_in)
-    targets = (conn, wave, mass, potential, levels, weights)
-    for k in range(6):
-        loads.append(pltpu.make_async_copy(sources[k], targets[k], load_sem.at[k]))
-        loads[k].start()
     chunks = wave.shape[1] // 256
     vectors = wave.shape[0]
     group = vectors + 8
@@ -195,13 +198,13 @@
     top_high = tops[vectors].astype(bf16).astype(f32)
     parts = jnp.where(lane >= 64, tops[vectors] - top_high, pltpu.roll(top_high, 64, 1))
     face[vectors // 2] = jnp.concatenate([parts, blank], axis=0).astype(bf16)
-    for k in range(3, 6):
-        loads[k].wait()
+    loads[3].wait()
+    loads[4].wait()
     exact = lax.Precision.HIGHEST
     size = 1.0 / jnp.left_shift(1, levels[...]).astype(f32)
     in_use = jnp.where(lane < live[0], 1.0, 0.0)
     volume = size * size * size / 8.0 * in_use
-    coefficient = volume * weights[:, 0:1] * potential[...]
+    coefficient = volume * node_weights() * potential[...]
     coefficient = jnp.dot(coefficient, order, precision=exact, preferred_element_type=f32)
     cell_out[:ROWS, :] = jnp.dot(spread, coefficient, precision=exact, preferred_element_type=f32)
     kinetic = jnp.broadcast_to(size / 4.0 * in_use, (8, 128))
@@ -233,7 +236,7 @@
     stiff = jnp.dot(stiffness, values, preferred_element_type=jnp.float32)
     coefficient, kinetic = cell_data[:ROWS], cell_data[ROWS:ROWS + 1]
     results = []
-    for part in range(2):
+    for part in range(len(pair)):
         columns = slice(128 * part, 128 * part + 128)
         low = values[:, columns].astype(jnp.float32)
         results.append(shared_sums(kinetic * stiff[:, columns] + coefficient * low))
@@ -244,7 +247,7 @@
     return (lax.div(peer, others), lax.rem(peer, others))
 
 
-def meet_all(me, count, others):
+def greet_all(me, count, others):
     barrier = pltpu.get_barrier_semaphore()
 
     def greet(k, carry):
@@ -255,7 +258,7 @@
         return carry
 
     lax.fori_loop(1, count, greet, 0)
-    pl.semaphore_wait(barrier, count - 1)
+    return barrier
 
 
 def wait_bytes(ref, semaphore):
@@ -263,9 +266,11 @@
 
 
 def filter_kernel(
-    rows_of, others, bounds, nodal_in, face_in, inverse_in, cell_in, stiffness_in, wave_in, earlier,
+    rows_of, others, bounds, live,
+    wave_in, mass_in, conn_in, potential_in, levels_in, stiffness_in, earlier,
     filtered, own_rows,
-    nodal, inverse, cell_data, stiffness, wave, sums, degree, edge, spread_out, rounded,
+    wave, mass_row, conn, potential, levels, stiffness, packed, low, high, stage,
+    nodal, face, inverse, cell_data, sums, degree, spread_out, rounded,
     ghost, above, below, above_again, bottoms, tops, bottoms_again,
     held, quarter, partial, to_send, received, own_low, gathered, low_rows,
     input_sem, load_sem, ghost_send, ghost_recv, up_send, up_recv, down_send, down_recv,
@@ -288,11 +293,17 @@
     center, halfwidth = bounds[0], bounds[1]
     lane = lane_iota((1, 128))
     inputs = []
-    sources = (nodal_in, cell_in, stiffness_in, inverse_in, wave_in)
-    targets = (nodal, cell_data, stiffness, inverse, wave)
-    for k in range(5):
+    sources = (conn_in, wave_in, mass_in, potential_in, levels_in, stiffness_in)
+    targets = (conn, wave, mass_row, potential, levels, stiffness)
+    for k in range(6):
         inputs.append(pltpu.make_async_copy(sources[k], targets[k], input_sem.at[k]))
         inputs[k].start()
+    loads = []
+    for k in range(parts):
+        here = pl.ds(pl.multiple_of(lax.rem(first_part + k, parts) * depth, depth), depth)
+        loads.append(pltpu.make_async_copy(earlier.at[here], held.at[here], load_sem.at[k]))
+        loads[k].start()
+    barrier = greet_all(me, count, others)
     has_above, has_below = along < rows_of - 1, along > 0
 
     def to_neighbour(source, target, step, send, recv):
@@ -301,17 +312,15 @@
             device_id=(along + step, mine), device_id_type=pl.DeviceIdType.MESH,
         )
 
-    meet_all(me, count, others)
+    gather_nodes(
+        live, wave, mass_row, conn, potential, levels, nodal, face, inverse, cell_data,
+        packed, low, high, stage, inputs,
+    )
+    pl.semaphore_wait(barrier, count - 1)
 
     @pl.when(has_above)
     def _():
-        to_neighbour(face_in, ghost, 1, ghost_send, ghost_recv).start()
-
-    loads = []
-    for k in range(parts):
-        here = pl.ds(pl.multiple_of(lax.rem(first_part + k, parts) * depth, depth), depth)
-        loads.append(pltpu.make_async_copy(earlier.at[here], held.at[here], load_sem.at[k]))
-        loads[k].start()
+        to_neighbour(face, ghost, 1, ghost_send, ghost_recv).start()
 
     @pl.when(jnp.logical_not(has_above))
     def _():
@@ -323,8 +332,7 @@
         below[...] = jnp.zeros_like(below)
         ghost[...] = jnp.zeros_like(ghost)
 
-    for k in range(5):
-        inputs[k].wait()
+    inputs[5].wait()
 
     @pl.when(has_below)
     def _():
@@ -338,96 +346,96 @@
         nodal[here, :] = jnp.where(lane < 64, value, nodal[here, :])
     blank = jnp.zeros((7, 128), f32)
 
-    def bottom_faces():
-        first, second = edge[pl.ds(0, 25, stride=8), :], edge[pl.ds(ROWS, 25, stride=8), :]
-        rows = jnp.where(lane < 64, first, pltpu.roll(second, 64, 1))
-        return jnp.concatenate([rows, blank], axis=0).astype(bf16)
-
-    def top_faces():
-        first, second = edge[pl.ds(4, 25, stride=8), :], edge[pl.ds(ROWS + 4, 25, stride=8), :]
-        rows = jnp.where(lane < 64, pltpu.roll(first, 64, 1), second)
-        return jnp.concatenate([rows, blank], axis=0).astype(bf16)
-
-    def add_above(faces):
+    def rows(v, first, size, stride):
+        return pl.ds(ROWS * v + first, size, stride=stride)
+
+    def bottom_faces(i):
+        first, second = sums[rows(2 * i, 0, 25, 8), :], sums[rows(2 * i + 1, 0, 25, 8), :]
+        joined = jnp.where(lane < 64, first, pltpu.roll(second, 64, 1))
+        return jnp.concatenate([joined, blank], axis=0).astype(bf16)
+
+    def top_faces(i):
+        first, second = sums[rows(2 * i, 4, 25, 8), :], sums[rows(2 * i + 1, 4, 25, 8), :]
+        joined = jnp.where(lane < 64, pltpu.roll(first, 64, 1), second)
+        return jnp.concatenate([joined, blank], axis=0).astype(bf16)
+
+    def add_above(i, faces):
         got = faces.astype(f32)[:25]
         for k, value in enumerate((pltpu.roll(got, 64, 1), got)):
-            edge[pl.ds(ROWS * k + 4, 25, stride=8), :] += jnp.where(lane >= 64, value, 0.0)
-
-    def add_below(faces):
+            sums[rows(2 * i + k, 4, 25, 8), :] += jnp.where(lane >= 64, value, 0.0)
+
+    def add_below(i, faces):
         got = faces.astype(f32)[:25]
         for k, value in enumerate((got, pltpu.roll(got, 64, 1))):
-            edge[pl.ds(ROWS * k, 25, stride=8), :] += jnp.where(lane < 64, value, 0.0)
-
-    def both_rows(i):
-        return pl.ds(pl.multiple_of(2 * ROWS * i, 16), 2 * ROWS)
-
-    def apply(values):
-        result = cell_operator(
-            [values[:ROWS], values[ROWS:]], stiffness[:ROWS, :ROWS], cell_data[...]
-        )
-        for k in range(2):
-            edge[ROWS * k:ROWS * k + ROWS, :] = result[k]
-
-    def first_step(i, carry):
-        apply(nodal[both_rows(i), :])
-        sums[both_rows(i), :] = edge[...]
-        bottoms[i] = bottom_faces()
-        tops[i] = top_faces()
+            sums[rows(2 * i + k, 0, 25, 8), :] += jnp.where(lane < 64, value, 0.0)
+
+    steps = pairs // 2
+
+    def vector(v):
+        return slice(ROWS * v, ROWS * v + ROWS)
+
+    def apply(g, values):
+        result = cell_operator(values, stiffness[:ROWS, :ROWS], cell_data[...])
+        for k in range(4):
+            sums[vector(4 * g + k), :] = result[k]
+
+    for g in range(steps):
+        both = pl.ds(2 * g, 2)
+        apply(g, [nodal[vector(4 * g + k), :] for k in range(4)])
+        for i in (2 * g, 2 * g + 1):
+            bottoms[i] = bottom_faces(i)
+            tops[i] = top_faces(i)
 
         @pl.when(has_below)
         def _():
-            to_neighbour(bottoms.at[i], above.at[i], -1, up_send, up_recv.at[i]).start()
+            to_neighbour(bottoms.at[both], above.at[both], -1, up_send, up_recv.at[g]).start()
 
         @pl.when(has_above)
         def _():
-            to_neighbour(tops.at[i], below.at[i], 1, down_send, down_recv.at[i]).start()
-
-        return carry
-
-    lax.fori_loop(0, pairs, first_step, 0)
+            to_neighbour(tops.at[both], below.at[both], 1, down_send, down_recv.at[g]).start()
+
     mass = nodal[ROWS * vectors:ROWS * vectors + ROWS, :]
-    squared = jnp.concatenate([mass * mass, mass * mass], axis=0)
-
-    def second_step(i, carry):
+    squared = mass * mass
+    for g in range(steps):
+        both = pl.ds(2 * g, 2)
+
         @pl.when(has_above)
         def _():
-            wait_bytes(above.at[i], up_recv.at[i])
+            wait_bytes(above.at[both], up_recv.at[g])
 
         @pl.when(has_below)
         def _():
-            wait_bytes(below.at[i], down_recv.at[i])
-
-        edge[...] = sums[both_rows(i), :]
-        add_above(above[i])
-        add_below(below[i])
-        one = (squared * edge[...] - center * nodal[both_rows(i), :]) / halfwidth
-        degree[both_rows(i), :] = one
-        apply(one)
-        sums[both_rows(i), :] = edge[...]
-        bottoms_again[i] = bottom_faces()
+            wait_bytes(below.at[both], down_recv.at[g])
+
+        for i in (2 * g, 2 * g + 1):
+            add_above(i, above[i])
+            add_below(i, below[i])
+        ones = []
+        for v in range(4 * g, 4 * g + 4):
+            ones.append((squared * sums[vector(v), :] - center * nodal[vector(v), :]) / halfwidth)
+            degree[vector(v), :] = ones[-1]
+        apply(g, ones)
+        for i in (2 * g, 2 * g + 1):
+            bottoms_again[i] = bottom_faces(i)
 
         @pl.when(has_below)
         def _():
             to_neighbour(
-                bottoms_again.at[i], above_again.at[i], -1, again_send, again_recv.at[i]
+                bottoms_again.at[both], above_again.at[both], -1, again_send, again_recv.at[g]
             ).start()
 
-        return carry
-
-    lax.fori_loop(0, pairs, second_step, 0)
     unscale = 1.0 / jnp.where(mass == 0.0, 1.0, mass)
-    for i in range(pairs):
+    for g in range(steps):
         @pl.when(has_above)
         def _():
-            wait_bytes(above_again.at[i], again_recv.at[i])
-
-        here = both_rows(i)
-        edge[...] = sums[here, :]
-        add_above(above_again[i])
-        two = 2.0 * (squared * edge[...] - center * degree[here, :]) / halfwidth - nodal[here, :]
-        for k in range(2):
-            v = 2 * i + k
-            block = blocks_of(two[ROWS * k:ROWS * k + ROWS] * unscale)
+            wait_bytes(above_again.at[pl.ds(2 * g, 2)], again_recv.at[g])
+
+        for i in (2 * g, 2 * g + 1):
+            add_above(i, above_again[i])
+        for v in range(4 * g, 4 * g + 4):
+            one = degree[vector(v), :]
+            two = 2.0 * (squared * sums[vector(v), :] - center * one) / halfwidth
+            block = blocks_of((two - nodal[vector(v), :]) * unscale)
             kept = [block[5 * a + b] for a in range(4) for b in range(4)]
             for n, part in enumerate(kept + list(pack_edges(block, 0.0))):
                 spread_out[pl.ds(4 * n * vectors + v, 4, stride=vectors), :] = part[1:5]
@@ -451,9 +459,9 @@
             product = product.reshape(GATHERED // 2, vectors, 256)
             total = jnp.sum(jnp.where(row_of == row[None], product, 0.0), axis=0)
             here = pl.ds(pl.multiple_of(chunk * 256, 256), 256)
-            vector = wave[:, here]
-            one = -center * vector / halfwidth
-            unused = -2.0 * center * one / halfwidth - vector
+            wanted = wave[:, here]
+            one = -center * wanted / halfwidth
+            unused = -2.0 * center * one / halfwidth - wanted
             rounded[:, here] = jnp.where(row_code < 0, unused, total).astype(bf16)
         source = rounded.at[:, pl.ds(pl.multiple_of(peer * width, 128), width)]
         if q < others - 1:
@@ -495,23 +503,28 @@
     own_rows[...] = jnp.concatenate([total[:, :columns], total[:, columns:]], axis=0)
     own_low[...] = total.astype(jnp.bfloat16)
     gathered[me] = own_low[...]
+    own_part = lax.div(me, blocks)
     for k in range(1, count):
         peer = lax.rem(me + k, count)
         pltpu.make_async_remote_copy(
-            own_low, gathered.at[me], all_send, all_recv,
+            own_low, gathered.at[me], all_send, all_recv.at[own_part],
             device_id=mesh_id(peer, others), device_id_type=pl.DeviceIdType.MESH,
         ).start()
-    wait_bytes(gathered.at[pl.ds(0, count - 1)], all_recv)
-    for k in range(count):
-        piece = gathered[k]
-        low_rows[share * k:share * k + half, :] = piece[:, :columns]
-        low_rows[share * k + half:share * k + share, :] = piece[:, columns:]
-    weights = low_rows[...].astype(jnp.float32).T.astype(jnp.bfloat16)
-    step = 256
-    for start in range(0, width, step):
-        here = slice(start, start + step)
-        taken = jnp.dot(weights, held[:, here], preferred_element_type=jnp.float32)
-        filtered[:, here] = vectors_here[:, here].astype(jnp.float32) - taken
+    for k in range(parts):
+        part = lax.rem(own_part + k, parts)
+        come = blocks - 1 if k == 0 else blocks
+        wait_bytes(gathered.at[pl.ds(0, come)], all_recv.at[part])
+        for t in range(blocks):
+            piece = gathered[part * blocks + t]
+            low_rows[share * t:share * t + half, :] = piece[:, :columns]
+            low_rows[share * t + half:share * t + share, :] = piece[:, columns:]
+        weights = low_rows[...].astype(jnp.float32).T.astype(jnp.bfloat16)
+        deep = pl.ds(pl.multiple_of(part * depth, depth), depth)
+        for start in range(0, width, 256):
+            here = slice(start, start + 256)
+            taken = jnp.dot(weights, held[deep, here], preferred_element_type=jnp.float32)
+            base = vectors_here[:, here].astype(jnp.float32) if k == 0 else filtered[:, here]
+            filtered[:, here] = base - taken
     wait_bytes(quarter.at[pl.ds(0, others - 1)], swap_send)
     wait_bytes(received, sum_send)
     wait_bytes(gathered.at[pl.ds(0, count - 1)], all_send)
@@ -525,55 +538,6 @@
     def _():
         wait_bytes(bottoms, up_send)
         wait_bytes(bottoms_again, again_send)
-
-
-def filter_block(bounds, nodal, face, inverse, cell_data, stiffness, wave_block, earlier_vectors):
-    along, others = lax.axis_size("cells"), lax.axis_size("vecs")
-    count = along * others
-    vectors, owned = wave_block.shape
-    depth, width = earlier_vectors.shape
-    share, columns = depth // count, vectors * others
-    bf16, f32 = jnp.bfloat16, jnp.float32
-    dma = pltpu.SemaphoreType.DMA
-    pairs = vectors // 2
-    faces = pltpu.VMEM((pairs, 32, 128), bf16)
-    block = (share // 2, 2 * columns)
-    return pl.pallas_call(
-        functools.partial(filter_kernel, along, others),
-        out_shape=(
-            jax.ShapeDtypeStruct((columns, width), f32),
-            jax.ShapeDtypeStruct((share, columns), f32),
-        ),
-        in_specs=[pl.BlockSpec(memory_space=pltpu.SMEM)] + [pl.BlockSpec(memory_space=pl.ANY)] * 7,
-        out_specs=(pl.BlockSpec(memory_space=pltpu.VMEM),) * 2,
-        scratch_shapes=[
-            pltpu.VMEM(nodal.shape, f32),
-            pltpu.VMEM(inverse.shape, f32),
-            pltpu.VMEM(cell_data.shape, f32),
-            pltpu.VMEM(stiffness.shape, bf16),
-            pltpu.VMEM((vectors, owned), f32),
-            pltpu.VMEM((vectors * ROWS, 128), f32),
-            pltpu.VMEM((vectors * ROWS, 128), f32),
-            pltpu.VMEM((2 * ROWS, 128), f32),
-            pltpu.VMEM((GATHERED * vectors, 128), f32),
-            pltpu.VMEM((vectors, owned), bf16),
-            pltpu.VMEM((pairs + 1, 32, 128), bf16),
-            faces, faces, faces, faces, faces, faces,
-            pltpu.VMEM((depth, width), bf16),
-            pltpu.VMEM((others, vectors, width), bf16),
-            pltpu.VMEM((count,) + block, f32),
-            pltpu.VMEM((count,) + block, bf16),
-            pltpu.VMEM((count - 1,) + block, bf16),
-            pltpu.VMEM(block, bf16),
-            pltpu.VMEM((count,) + block, bf16),
-            pltpu.VMEM((depth, columns), bf16),
-            dma((5,)), dma((4,)), dma, dma, dma, dma((pairs,)), dma, dma((pairs,)),
-            dma, dma((pairs,)), dma, dma, dma, dma, dma, dma,
-        ],
-        compiler_params=pltpu.CompilerParams(
-            collective_id=0, has_side_effects=True, vmem_limit_bytes=VMEM_BYTES
-        ),
-    )(bounds, nodal, face, inverse, cell_data, stiffness, wave_block, earlier_vectors)
 
 
 def per_device(
@@ -588,44 +552,68 @@
     halfwidth,
     earlier_vectors,
 ):
-    stiffness, quadrature = fixed_tables()
+    stiffness, _ = fixed_tables()
     stiffness = jnp.asarray(stiffness).astype(jnp.bfloat16)
-    weights = jnp.asarray(np.broadcast_to(quadrature[:, None], (125, 128)))
+    along, others = lax.axis_size("cells"), lax.axis_size("vecs")
+    count = along * others
     vectors, owned = wave_block.shape
     nodes, cells = connectivity.shape
-    group = vectors + 8
-    f32, bf16 = jnp.float32, jnp.bfloat16
-    shape = jax.ShapeDtypeStruct
-    whole = pl.BlockSpec(memory_space=pltpu.VMEM)
-    nodal, face, inverse, cell_data = pl.pallas_call(
-        gather_kernel,
+    depth, width = earlier_vectors.shape
+    share, columns = depth // count, vectors * others
+    group, pairs = vectors + 8, vectors // 2
+    parts, steps = 4, vectors // 4
+    bf16, f32 = jnp.bfloat16, jnp.float32
+    dma = pltpu.SemaphoreType.DMA
+    faces = pltpu.VMEM((pairs, 32, 128), bf16)
+    all_faces = pltpu.VMEM((pairs + 1, 32, 128), bf16)
+    block = (share // 2, 2 * columns)
+    return pl.pallas_call(
+        functools.partial(filter_kernel, along, others),
         out_shape=(
-            shape(((vectors + 1) * ROWS, 128), f32),
-            shape((vectors // 2 + 1, 32, 128), bf16),
-            shape((80, 256), f32),
-            shape((208, 128), f32),
+            jax.ShapeDtypeStruct((columns, width), f32),
+            jax.ShapeDtypeStruct((share, columns), f32),
         ),
-        in_specs=[pl.BlockSpec(memory_space=pltpu.SMEM)] + [pl.BlockSpec(memory_space=pl.ANY)] * 6,
-        out_specs=(whole,) * 4,
+        in_specs=[pl.BlockSpec(memory_space=pltpu.SMEM)] * 2
+        + [pl.BlockSpec(memory_space=pl.ANY)] * 7,
+        out_specs=(pl.BlockSpec(memory_space=pltpu.VMEM),) * 2,
         scratch_shapes=[
             pltpu.VMEM((vectors, owned), f32),
             pltpu.VMEM((1, owned), f32),
             pltpu.VMEM((nodes, cells), jnp.int32),
             pltpu.VMEM((nodes, cells), f32),
             pltpu.VMEM((1, cells), jnp.int32),
-            pltpu.VMEM((nodes, 128), f32),
+            pltpu.VMEM(stiffness.shape, bf16),
             pltpu.VMEM((group * owned // 256, 256), f32),
             pltpu.VMEM((ROWS + 16, 128), jnp.int32),
             pltpu.VMEM((ROWS + 16, 128), jnp.int32),
             pltpu.VMEM(((ROWS + 16) * group, 128), f32),
-            pltpu.SemaphoreType.DMA((6,)),
+            pltpu.VMEM(((vectors + 1) * ROWS, 128), f32),
+            all_faces,
+            pltpu.VMEM((80, 256), f32),
+            pltpu.VMEM((ROWS + 8, 128), f32),
+            pltpu.VMEM((vectors * ROWS, 128), f32),
+            pltpu.VMEM((vectors * ROWS, 128), f32),
+            pltpu.VMEM((GATHERED * vectors, 128), f32),
+            pltpu.VMEM((vectors, owned), bf16),
+            all_faces,
+            faces, faces, faces, faces, faces, faces,
+            pltpu.VMEM((depth, width), bf16),
+            pltpu.VMEM((others, vectors, width), bf16),
+            pltpu.VMEM((count,) + block, f32),
+            pltpu.VMEM((count,) + block, bf16),
+            pltpu.VMEM((count - 1,) + block, bf16),
+            pltpu.VMEM(block, bf16),
+            pltpu.VMEM((count,) + block, bf16),
+            pltpu.VMEM((depth // parts, columns), bf16),
+            dma((6,)), dma((parts,)), dma, dma, dma, dma((steps,)), dma, dma((steps,)),
+            dma, dma((steps,)), dma, dma, dma, dma, dma, dma((parts,)),
         ],
-        compiler_params=pltpu.CompilerParams(vmem_limit_bytes=VMEM_BYTES),
-    )(live_cells, wave_block, mass_scale[None], connectivity, potential, levels[None], weights)
-    bounds = jnp.stack([center, halfwidth])
-    share = earlier_vectors.shape[0] // lax.axis_size(("cells", "vecs"))
-    return filter_block(
-        bounds, nodal, face, inverse, cell_data, stiffness, wave_block, earlier_vectors
+        compiler_params=pltpu.CompilerParams(
+            collective_id=0, has_side_effects=True, vmem_limit_bytes=VMEM_BYTES
+        ),
+    )(
+        jnp.stack([center, halfwidth]), live_cells, wave_block, mass_scale[None], connectivity,
+        potential, levels[None], stiffness, earlier_vectors,
     )
 
 

time: 72.2 us -> 60.6 us (0.84)
  local copies, waits for them, and re-layouts: 10.9 us -> 3.29 us
  Pallas kernels: 58.2 us -> 53.5 us
    unnamed x16 -> x2, local copies, waits for them, and re-layouts: 10.2 us -> 3.29 us
    pallas_call x2 -> x1, Pallas kernels: 58.2 us -> 53.5 us  [per_device(): pl.pallas_call(functools.partial(filter_kernel, along, others), out_shape...]
    another operation x1 -> x0, local copies, waits for them, and re-layouts: 0.73 us -> none
where the time goes in v4:
time: 60.6 us; the launch traced here: 59.9 us
  Pallas kernels  53.5 us (88%)
  local copies, waits for them, and re-layouts  3.29 us (5%)
  between operations  2.58 us (4%)
    pallas_call x1, Pallas kernels, per_device(): pl.pallas_call(functools.partial(filter_kernel, along, others), out_shape...  53.5 us
    unnamed x2, local copies, waits for them, and re-layouts  3.29 us

profile of v4, /device:TPU:0, one launch (start us, length us, event | category | flops | bytes accessed | tf_op | source)
XLA Modules:
  0.0 59.9 jit_solution(5225056301903223783)
XLA Ops:
  2.6 0.6 pad_maximum_fusion.bounds
  3.1 53.5 %shard_map.113 = (f32[64,2304]{1,0:T(8,128)}, f32[64,64]{1,0:T(8,128)}) custom-call(f32[2]{0:T(128)} %pad_maximum_fusion.bounds, s32[1]{0:T(128)S(6)} %copy.14.live, f32[16,9216]{1,0:T(8,128)} %wave_in.1, f32[1,9216]{1,0:T(1,128)} %bitcast.6, s32[125,128]{1,0:T(8,128)} %conn_in.1, f32[125,128]{1,0:T(8,128)} %potential_in.1, s32[1,128]{1,0:T(1,128)} %bitcast.7, ...), custom_call_target="tpu_custom_call" | custom-call | tf_op jit(solution)/shard_map/pallas_call | solution.py:570
  56.6 1.9 %copy.17 = f32[64,2304]{1,0:T(8,128)} copy(f32[64,2304]{1,0:T(8,128)} %get-tuple-element.4) | data formatting | bytes 1179648
  58.6 1.4 %copy.18 = f32[64,64]{1,0:T(8,128)} copy(f32[64,64]{1,0:T(8,128)} %get-tuple-element.5) | data formatting | bytes 32768
